TPU v7x, 32 devices: a whole 2x2x4 slice. The times are simulated.
32 devices in a mesh: dp: 8 (over z, x), tensor: 4 (over y, core).
Axes of the slice: x: 2, y: 2, z: 4, core: 2. Of those that a mesh axis runs over, the one named last changes fastest.
Arguments:
- tokens: bfloat16 [32768, 1024], P('dp'), may hold values from -6 to 6
- lengths: int32 [64], P('dp'), may hold values from 1 to 512, 24576 in all
- qkv_weight: bfloat16 [3, 1024, 1024], P(None, 'dp', 'tensor'), may hold values from -0.1875 to 0.1875
- qv_bias: bfloat16 [2, 16, 64], P(None, 'tensor', 'dp'), may hold values from -2 to 2
- out_weight: bfloat16 [1024, 1024], P('tensor', 'dp'), may hold values from -2 to 2
- out_bias: bfloat16 [1024], P('dp'), may hold values from -2 to 2
- up_weight: bfloat16 [1024, 4096], P('dp', 'tensor'), may hold values from -0.1875 to 0.1875
- up_bias: bfloat16 [64, 64], P('tensor', 'dp'), may hold values from -3 to 3
- down_weight: bfloat16 [4096, 1024], P('tensor', 'dp'), may hold values from -0.09375 to 0.09375
- down_bias: bfloat16 [1024], P('dp'), may hold values from -2 to 2
- norm_gain: bfloat16 [2, 1024], P(None, 'dp'), may hold values from 0.5 to 1.5
- norm_shift: bfloat16 [2, 1024], P(None, 'dp'), may hold values from -2 to 2
- cotangent: bfloat16 [32768, 1024], P('dp'), may hold values from -6 to 6
Outputs:
- out: bfloat16 [32768, 1024], P(('dp', 'tensor'))
- in_grad: float32 [32768, 1024], P(('dp', 'tensor'))
- qkv_weight_grad: float32 [3, 1024, 1024], P(None, 'dp', 'tensor')
- qv_bias_grad: float32 [2, 16, 64], P(None, 'tensor', 'dp')
- out_weight_grad: float32 [1024, 1024], P('tensor', 'dp')
- out_bias_grad: float32 [1024], P('dp')
- up_weight_grad: float32 [1024, 4096], P('dp', 'tensor')
- up_bias_grad: float32 [64, 64], P('tensor', 'dp')
- down_weight_grad: float32 [4096, 1024], P('tensor', 'dp')
- down_bias_grad: float32 [1024], P('dp')
- norm_gain_grad: float32 [2, 1024], P(None, 'dp')
- norm_shift_grad: float32 [2, 1024], P(None, 'dp')
All inputs are finite; a program needn't handle non-finite values. No bound on the sum of `lengths` on one device may be relied on, other than what follows from the above.
Results may differ from a plain program's by a relative error of at most 0.02.
Values may be sent and summed in bfloat16 or wider, within the bound.
A program may use at most 320 MiB of HBM per device.

v0:
```python
import jax
import jax.numpy as jnp
from jax import lax
from jax.sharding import PartitionSpec as P

HD = 64
SEQ = 512


EPSILON = 1e-05


def row_stats(summed):
    row_mean = jnp.mean(summed, axis=-1, keepdims=True)
    centred = summed - row_mean
    inverse = lax.rsqrt(jnp.mean(centred * centred, axis=-1, keepdims=True) + EPSILON)
    return (centred * inverse, inverse[:, 0])


def norm_back(grad_rows, unit_rows, inverse, gain_row):
    scaled = grad_rows * gain_row
    inner = (
        scaled
        - jnp.mean(scaled, axis=-1, keepdims=True)
        - unit_rows * jnp.mean(scaled * unit_rows, axis=-1, keepdims=True)
    )
    return (
        inverse[:, None] * inner,
        jnp.sum(grad_rows * unit_rows, axis=0),
        jnp.sum(grad_rows, axis=0),
    )


def masked_scores(queries, key_heads, key_valid, scale):
    scores = (
        jnp.einsum("sihe,sjhe->shij", queries, key_heads, preferred_element_type=jnp.float32)
        * scale
    )
    return jnp.where(key_valid[:, None, None, :] > 0, scores, -1000000000.0)


def attend(queries, key_heads, values, key_valid, scale):
    scores = masked_scores(queries, key_heads, key_valid, scale)
    top_score = jnp.max(scores, axis=-1, keepdims=True)
    expo = jnp.exp(scores - top_score)
    total = jnp.sum(expo, axis=-1, keepdims=True)
    attention = (expo / total).astype(jnp.bfloat16)
    context = jnp.einsum("shij,sjhe->sihe", attention, values, preferred_element_type=jnp.float32)
    return (context, top_score + jnp.log(total))


def attend_back(queries, key_heads, values, key_valid, log_total, d_context, scale):
    scores = masked_scores(queries, key_heads, key_valid, scale)
    attention = jnp.exp(scores - log_total)
    d_probs = jnp.einsum("sihe,sjhe->shij", d_context, values, preferred_element_type=jnp.float32)
    d_scores = (
        attention * (d_probs - jnp.sum(attention * d_probs, axis=-1, keepdims=True))
    ).astype(jnp.bfloat16)
    d_query = (
        jnp.einsum("shij,sjhe->sihe", d_scores, key_heads, preferred_element_type=jnp.float32)
        * scale
    ).astype(jnp.bfloat16)
    d_key = (
        jnp.einsum("shij,sihe->sjhe", d_scores, queries, preferred_element_type=jnp.float32) * scale
    ).astype(jnp.bfloat16)
    d_value = jnp.einsum(
        "shij,sihe->sjhe",
        attention.astype(jnp.bfloat16),
        d_context,
        preferred_element_type=jnp.float32,
    ).astype(jnp.bfloat16)
    return (d_query, d_key, d_value)


def joined_weight(qkv_local):
    return jnp.transpose(qkv_local, (1, 0, 2)).reshape(qkv_local.shape[1], 3 * qkv_local.shape[2])


def per_device(
    tokens,
    lengths,
    qkv_weight,
    qv_bias,
    out_weight,
    out_bias,
    up_weight,
    up_bias,
    down_weight,
    down_bias,
    norm_gain,
    norm_shift,
    cotangent,
):
    (
        qkv_full,
        qv_full,
        out_full,
        outb_full,
        up_full,
        upb_full,
        down_full,
        downb_full,
        gain_full,
        shift_full,
    ) = (
        lax.all_gather(qkv_weight, "dp", axis=1, tiled=True),
        lax.all_gather(qv_bias, "dp", axis=2, tiled=True),
        lax.all_gather(out_weight, "dp", axis=1, tiled=True),
        lax.all_gather(out_bias, "dp", axis=0, tiled=True),
        lax.all_gather(up_weight, "dp", axis=0, tiled=True),
        lax.all_gather(up_bias, "dp", axis=1, tiled=True),
        lax.all_gather(down_weight, "dp", axis=1, tiled=True),
        lax.all_gather(down_bias, "dp", axis=0, tiled=True),
        lax.all_gather(norm_gain, "dp", axis=1, tiled=True),
        lax.all_gather(norm_shift, "dp", axis=1, tiled=True),
    )
    token_count = tokens.shape[0]
    width = qkv_full.shape[1]
    head_width = qkv_full.shape[2]
    seq_count = token_count // SEQ
    local_heads = head_width // HD
    scale = HD ** (-0.5)
    gains = gain_full.astype(jnp.float32)
    shifts = shift_full.astype(jnp.float32)
    out_shift = outb_full.astype(jnp.float32)
    down_shift = downb_full.astype(jnp.float32)
    share_rows = token_count // lax.axis_size("tensor")
    start_row = lax.axis_index("tensor") * share_rows
    joined = joined_weight(qkv_full)
    projected = jnp.dot(tokens, joined, preferred_element_type=jnp.float32)
    qv_flat = qv_full.reshape(2, head_width).astype(jnp.float32)
    queries = (projected[:, :head_width] + qv_flat[0]).astype(jnp.bfloat16)
    key_heads = projected[:, head_width : 2 * head_width].astype(jnp.bfloat16)
    values = (projected[:, 2 * head_width :] + qv_flat[1]).astype(jnp.bfloat16)
    head_shape = (seq_count, SEQ, local_heads, HD)
    positions = lax.iota(jnp.int32, SEQ)
    key_valid = (positions[None, :] < lengths[:, None]).astype(jnp.int32)
    row_valid = key_valid.reshape(token_count).astype(jnp.float32)
    context, log_total = attend(
        queries.reshape(head_shape),
        key_heads.reshape(head_shape),
        values.reshape(head_shape),
        key_valid,
        scale,
    )
    context_b = context.reshape(token_count, head_width).astype(jnp.bfloat16)
    attn_part = jnp.dot(context_b, out_full, preferred_element_type=jnp.float32)
    attended = lax.psum(attn_part.astype(jnp.bfloat16), "tensor").astype(jnp.float32)
    unit_one, inverse_one = row_stats(tokens.astype(jnp.float32) + attended + out_shift)
    normed_one = unit_one * gains[0] + shifts[0]
    normed_one_b = normed_one.astype(jnp.bfloat16)
    pre_act = jnp.dot(normed_one_b, up_full, preferred_element_type=jnp.float32) + upb_full.reshape(
        -1
    ).astype(jnp.float32)
    hidden_b = jax.nn.gelu(pre_act, approximate=False).astype(jnp.bfloat16)
    ffn_part = jnp.dot(hidden_b, down_full, preferred_element_type=jnp.float32)
    ffn_out = lax.psum(ffn_part.astype(jnp.bfloat16), "tensor").astype(jnp.float32)
    unit_two, inverse_two = row_stats(normed_one + ffn_out + down_shift)
    out_rows = (unit_two * gains[1] + shifts[1]).astype(jnp.bfloat16)
    out = lax.dynamic_slice_in_dim(out_rows, start_row, share_rows, 0)
    qkv_back, out_back, up_back, down_back, gain_back = (
        lax.all_gather(qkv_weight, "dp", axis=1, tiled=True),
        lax.all_gather(out_weight, "dp", axis=1, tiled=True),
        lax.all_gather(up_weight, "dp", axis=0, tiled=True),
        lax.all_gather(down_weight, "dp", axis=1, tiled=True),
        lax.all_gather(norm_gain, "dp", axis=1, tiled=True),
    )
    joined_back = joined_weight(qkv_back)
    gains_back = gain_back.astype(jnp.float32)
    d_out = cotangent.astype(jnp.float32) * row_valid[:, None]
    d_sum_two, gain_two, shift_two = norm_back(d_out, unit_two, inverse_two, gains_back[1])
    d_ffn = d_sum_two.astype(jnp.bfloat16)
    down_bias_grad = jnp.sum(d_sum_two, axis=0)
    down_grad = jnp.einsum("rf,rd->fd", hidden_b, d_ffn, preferred_element_type=jnp.float32)
    d_hidden = jnp.einsum("rd,fd->rf", d_ffn, down_back, preferred_element_type=jnp.float32)
    gelu_out, gelu_pull = jax.vjp(
        lambda inner_act: jax.nn.gelu(inner_act, approximate=False), pre_act
    )
    d_pre = gelu_pull(d_hidden)[0].astype(jnp.bfloat16)
    up_bias_grad = jnp.sum(d_pre.astype(jnp.float32), axis=0).reshape(upb_full.shape)
    up_grad = jnp.einsum("rd,rf->df", normed_one_b, d_pre, preferred_element_type=jnp.float32)
    back_part = jnp.einsum("rf,df->rd", d_pre, up_back, preferred_element_type=jnp.float32)
    d_normed_one = d_sum_two + lax.psum(back_part.astype(jnp.bfloat16), "tensor").astype(
        jnp.float32
    )
    d_sum_one, gain_one, shift_one = norm_back(d_normed_one, unit_one, inverse_one, gains_back[0])
    d_attn = d_sum_one.astype(jnp.bfloat16)
    out_bias_grad = jnp.sum(d_sum_one, axis=0)
    out_grad = jnp.einsum("rk,rd->kd", context_b, d_attn, preferred_element_type=jnp.float32)
    d_context = jnp.einsum(
        "rd,kd->rk", d_attn, out_back, preferred_element_type=jnp.float32
    ).astype(jnp.bfloat16)
    d_query, d_key, d_value = attend_back(
        queries.reshape(head_shape),
        key_heads.reshape(head_shape),
        values.reshape(head_shape),
        key_valid,
        log_total,
        d_context.reshape(head_shape),
        scale,
    )
    d_query = d_query.reshape(token_count, head_width)
    d_key = d_key.reshape(token_count, head_width)
    d_value = d_value.reshape(token_count, head_width)
    qv_bias_grad = jnp.stack(
        [jnp.sum(d_query.astype(jnp.float32), axis=0), jnp.sum(d_value.astype(jnp.float32), axis=0)]
    ).reshape(qv_full.shape)
    d_joined = jnp.concatenate([d_query, d_key, d_value], axis=1)
    qkv_grad = jnp.transpose(
        jnp.einsum("rd,rc->dc", tokens, d_joined, preferred_element_type=jnp.float32).reshape(
            width, 3, head_width
        ),
        (1, 0, 2),
    )
    in_part = jnp.einsum("rc,dc->rd", d_joined, joined_back, preferred_element_type=jnp.float32)
    gain_grad = jnp.stack([gain_one, gain_two])
    shift_grad = jnp.stack([shift_one, shift_two])
    in_rows = d_sum_one + lax.psum(in_part.astype(jnp.bfloat16), "tensor").astype(jnp.float32)
    in_grad = lax.dynamic_slice_in_dim(in_rows, start_row, share_rows, 0)
    (
        qkv_owned,
        qv_owned,
        out_owned,
        outb_owned,
        up_owned,
        upb_owned,
        down_owned,
        downb_owned,
        gain_owned,
        shift_owned,
    ) = (
        lax.psum_scatter(
            qkv_grad.astype(jnp.bfloat16), "dp", scatter_dimension=1, tiled=True
        ).astype(jnp.float32),
        lax.psum_scatter(
            qv_bias_grad.astype(jnp.bfloat16), "dp", scatter_dimension=2, tiled=True
        ).astype(jnp.float32),
        lax.psum_scatter(
            out_grad.astype(jnp.bfloat16), "dp", scatter_dimension=1, tiled=True
        ).astype(jnp.float32),
        lax.psum_scatter(
            out_bias_grad.astype(jnp.bfloat16), "dp", scatter_dimension=0, tiled=True
        ).astype(jnp.float32),
        lax.psum_scatter(
            up_grad.astype(jnp.bfloat16), "dp", scatter_dimension=0, tiled=True
        ).astype(jnp.float32),
        lax.psum_scatter(
            up_bias_grad.astype(jnp.bfloat16), "dp", scatter_dimension=1, tiled=True
        ).astype(jnp.float32),
        lax.psum_scatter(
            down_grad.astype(jnp.bfloat16), "dp", scatter_dimension=1, tiled=True
        ).astype(jnp.float32),
        lax.psum_scatter(
            down_bias_grad.astype(jnp.bfloat16), "dp", scatter_dimension=0, tiled=True
        ).astype(jnp.float32),
        lax.psum_scatter(
            gain_grad.astype(jnp.bfloat16), "dp", scatter_dimension=1, tiled=True
        ).astype(jnp.float32),
        lax.psum_scatter(
            shift_grad.astype(jnp.bfloat16), "dp", scatter_dimension=1, tiled=True
        ).astype(jnp.float32),
    )
    return (
        out,
        in_grad,
        qkv_owned,
        qv_owned,
        out_owned,
        outb_owned,
        up_owned,
        upb_owned,
        down_owned,
        downb_owned,
        gain_owned,
        shift_owned,
    )


def solution(mesh):
    in_specs = (
        P("dp", None),
        P("dp"),
        P(None, "dp", "tensor"),
        P(None, "tensor", "dp"),
        P("tensor", "dp"),
        P("dp"),
        P("dp", "tensor"),
        P("tensor", "dp"),
        P("tensor", "dp"),
        P("dp"),
        P(None, "dp"),
        P(None, "dp"),
        P("dp", None),
    )
    out_specs = (
        P(("dp", "tensor"), None),
        P(("dp", "tensor"), None),
        P(None, "dp", "tensor"),
        P(None, "tensor", "dp"),
        P("tensor", "dp"),
        P("dp"),
        P("dp", "tensor"),
        P("tensor", "dp"),
        P("tensor", "dp"),
        P("dp"),
        P(None, "dp"),
        P(None, "dp"),
    )
    return jax.shard_map(
        per_device, mesh=mesh, in_specs=in_specs, out_specs=out_specs, check_vma=False
    )
```

profile of v0, /device:TPU:0, one launch (start us, length us, event | category | flops | bytes accessed | tf_op | source)
XLA Modules:
  0.0 1431.9 jit_solution(2224479141743927063)
XLA Ops:
  9.8 32.4 %all_gather.36 = bf16[2,4,64]{1,0,2:T(2,128)(2,1)S(1)} all-gather(bf16[2,4,8]{1,0,2:T(2,128)(2,1)S(1)} %copy.142), channel_id=1, replica_groups=mesh['dp'=8,'tensor'=4] {'dp'}, dimensions={2}, use_global_device_ids=true | all-gather | bytes 1152 | tf_op jit(solution)/shard_map/all_gather | solution.py:107
  44.0 28.9 %all_gather.37 = bf16[256,1024]{1,0:T(8,128)(2,1)S(1)} all-gather(bf16[256,128]{1,0:T(8,128)(2,1)} %param.17), channel_id=1, replica_groups=mesh['dp'=8,'tensor'=4] {'dp'}, dimensions={1}, use_global_device_ids=true | all-gather | bytes 589824 | tf_op jit(solution)/shard_map/all_gather | solution.py:108
  72.9 9.8 fusion.63
  95.1 7.3 reshape.206
  102.4 6.9 copy.149
  109.3 7.1 reshape.204
  116.4 6.9 copy.150
  123.3 15.5 %fusion.16 = (f32[8,4,512]{2,1,0:T(4,128)S(1)}, f32[8,4,512,512]{2,3,1,0:T(8,128)}) fusion(pred[8,512]{1,0:T(8,128)(4,1)S(1)} %get-tuple-element.98, bf16[8,512,4,64]{1,3,2,0:T(8,128)(2,1)S(1)} %copy.148, bf16[8,512,4,64]{1,3,2,0:T(8,128)(2,1)} %copy.149), kind=kOutput, calls=%fused_computation.48 | convolution fusion | flops 1098891264 | bytes 37818368 | tf_op jit(solution)/shard_map/sihe,sjhe->shij/dot_general | solution.py:36
  138.9 14.9 %fusion = f32[8,4,512]{2,1,0:T(4,128)S(1)} fusion(f32[8,4,512]{2,1,0:T(4,128)S(1)} %get-tuple-element.100, f32[8,4,512,512]{2,3,1,0:T(8,128)} %get-tuple-element.101, pred[8,512]{1,0:T(8,128)(4,1)S(1)} %get-tuple-element.98), kind=kLoop, calls=%fused_computation.6 | loop fusion | flops 33538048 | bytes 33689600 | tf_op jit(solution)/shard_map/reduce_sum | solution.py:46
  153.9 14.9 %convert_bitcast_fusion.1 = bf16[8,512,4,64]{1,3,2,0:T(8,128)(2,1)S(1)} fusion(bf16[8,512,4,64]{1,3,2,0:T(8,128)(2,1)S(1)} %copy-done.7, f32[8,4,512]{2,1,0:T(4,128)S(1)} %fusion, f32[8,4,512]{2,1,0:T(4,128)S(1)} %get-tuple-element.100, f32[8,4,512,512]{2,3,1,0:T(8,128)} %get-tuple-element.101, pred[8,512]{1,0:T(8,128)(4,1)S(1)} %get-tuple-element.98), kind=kOutput, calls=%fused_computation.76 | convolution fusion | flops 1116733440 | bytes 37883904 | tf_op jit(solution)/shard_map/shij,sjhe->sihe/dot_general | solution.py:48
  179.2 19.1 %all-gather = bf16[8,1,128]{2,1,0:T(2,128)(2,1)S(1)} all-gather(bf16[1,1,128]{2,1,0:T(2,128)(2,1)S(1)} %bitcast.155), channel_id=1, replica_groups=mesh['dp'=8,'tensor'=4] {'dp'}, dimensions={0}, use_global_device_ids=true | all-gather | bytes 2304 | tf_op jit(solution)/shard_map/all_gather | solution.py:109
  198.2 16.2 %all_gather.39 = bf16[2,1024]{1,0:T(2,128)(2,1)S(1)} all-gather(bf16[2,128]{1,0:T(2,128)(2,1)S(1)} %copy-done.26), channel_id=1, replica_groups=mesh['dp'=8,'tensor'=4] {'dp'}, dimensions={1}, use_global_device_ids=true | all-gather | bytes 4608 | tf_op jit(solution)/shard_map/all_gather | solution.py:114
  214.4 18.2 %all_gather.40 = bf16[2,1024]{1,0:T(2,128)(2,1)S(1)} all-gather(bf16[2,128]{1,0:T(2,128)(2,1)S(1)} %copy-done.27), channel_id=1, replica_groups=mesh['dp'=8,'tensor'=4] {'dp'}, dimensions={1}, use_global_device_ids=true | all-gather | bytes 4608 | tf_op jit(solution)/shard_map/all_gather | solution.py:115
  233.7 26.0 %all_gather.42 = bf16[16,64]{0,1:T(8,128)(2,1)S(1)} all-gather(bf16[16,8]{0,1:T(8,128)(2,1)S(1)} %copy-done.23), channel_id=1, replica_groups=mesh['dp'=8,'tensor'=4] {'dp'}, dimensions={1}, use_global_device_ids=true | all-gather | bytes 2304 | tf_op jit(solution)/shard_map/all_gather | solution.py:111
  259.9 70.6 %all-reduce.10.cloned.1.call-done = bf16[4096,1024]{1,0:T(8,128)(2,1)} async-done(((bf16[4096,1024]{1,0:T(8,128)(2,1)}), bf16[4096,1024]{1,0:T(8,128)(2,1)}) %all-reduce.10.cloned.1.call-update) | async-done | bytes 8388624 | tf_op jit(solution)/shard_map/psum | solution.py:148
  330.5 8.6 fusion.17
  339.1 8.4 multiply_reduce_fusion.6
  347.5 34.6 %all-gather.8.cloned.1.call-done = bf16[1024,1024]{1,0:T(8,128)(2,1)} async-done(((bf16[128,1024]{1,0:T(8,128)(2,1)}), bf16[1024,1024]{1,0:T(8,128)(2,1)}) %all-gather.8.cloned.1.call-update) | async-done | bytes 2097168 | tf_op jit(solution)/shard_map/all_gather | solution.py:110
  382.1 50.2 %multiply_convert_fusion.1 = (bf16[4096,1024]{1,0:T(8,128)(2,1)}, f32[4096,1024]{1,0:T(8,128)}, f32[4096,1024]{1,0:T(8,128)}) fusion(f32[1024]{0:T(1024)S(1)} %reshape.181, bf16[1024,1024]{1,0:T(8,128)(2,1)} %all-gather.8.cloned.1.call-done, f32[1024]{0:T(1024)S(1)} %bitcast.142, f32[1024]{0:T(1024)S(1)} %bitcast.131, f32[4096]{0:T(1024)S(1)} %add_rsqrt_fusion.1, ...), kind=kOutput, calls=%fused_computation.26 | convolution fusion | flops 8904507392 | bytes 60866560 | tf_op jit(solution)/shard_map/dot_general | solution.py:152
  433.6 14.9 %convolution_convert_fusion.2 = bf16[4096,1024]{1,0:T(8,128)(2,1)} fusion(bf16[4096,1024]{1,0:T(8,128)(2,1)} %get-tuple-element.88, bf16[1024,1024]{1,0:T(8,128)(2,1)} %all-gather.10.cloned.1.call-done), kind=kOutput, calls=%fused_computation.52 | convolution fusion | flops 8594128896 | bytes 18874368 | tf_op jit(solution)/shard_map/dot_general | solution.py:156
  448.6 17.6 %all-gather.1 = bf16[8,1,128]{2,1,0:T(2,128)(2,1)S(1)} all-gather(bf16[1,1,128]{2,1,0:T(2,128)(2,1)S(1)} %bitcast.156), channel_id=1, replica_groups=mesh['dp'=8,'tensor'=4] {'dp'}, dimensions={0}, use_global_device_ids=true | all-gather | bytes 2304 | tf_op jit(solution)/shard_map/all_gather | solution.py:113
  466.2 133.6 %all-reduce.12.cloned.1.call-done = bf16[4096,1024]{1,0:T(8,128)(2,1)} async-done(((bf16[4096,1024]{1,0:T(8,128)(2,1)}), bf16[4096,1024]{1,0:T(8,128)(2,1)}) %all-reduce.12.cloned.1.call-update) | async-done | bytes 8388624 | tf_op jit(solution)/shard_map/psum | solution.py:157
  599.8 12.6 fusion.48
  612.4 12.7 multiply_reduce_fusion.5
  625.3 19.0 %multiply_reduce_fusion.1 = (bf16[1024]{0:T(1024)(128)(2,1)S(1)}, f32[4096]{0:T(1024)S(1)}, f32[4096]{0:T(1024)S(1)}, bf16[1024]{0:T(1024)(128)(2,1)S(1)}, f32[4096,1024]{1,0:T(8,128)S(1)}) fusion(bf16[4096,1024]{1,0:T(8,128)(2,1)} %param.25, f32[4096]{0:T(1024)S(1)} %bitcast.129, f32[1024]{0:T(1024)S(1)} %bitcast.147, f32[4096]{0:T(1024)S(1)} %add_rsqrt_fusion, ...), kind=kLoop, calls=%fused_computation.11 | loop fusion | flops 92264448 | bytes 50470912 | tf_op jit(solution)/shard_map/reduce_sum | solution.py:29
  644.3 13.6 subtract_multiply_fusion.1
  658.1 26.7 %fusion.62 = (bf16[1024]{0:T(1024)(128)(2,1)}, bf16[4096,1024]{1,0:T(8,128)(2,1)}) fusion(f32[4096,1024]{1,0:T(8,128)} %get-tuple-element.89, bf16[1024,1024]{1,0:T(8,128)(2,1)} %all-gather.10.cloned.1.call-done, f32[4096,1024]{1,0:T(8,128)} %subtract_multiply_fusion.1, f32[4096,1024]{1,0:T(8,128)} %get-tuple-element.102, f32[1024]{0:T(1024)S(1)} %reshape.181), kind=kOutput, calls=%fused_computation.118 | convolution fusion | flops 8661236736 | bytes 60823552 | tf_op jit(solution)/shard_map/rd,fd->rf/dot_general | solution.py:175
  684.8 14.9 %convolution_convert_fusion.1 = bf16[4096,1024]{1,0:T(8,128)(2,1)} fusion(bf16[4096,1024]{1,0:T(8,128)(2,1)} %get-tuple-element.110, bf16[1024,1024]{1,0:T(8,128)(2,1)S(1)} %copy-done.29), kind=kOutput, calls=%fused_computation.51 | convolution fusion | flops 8594128896 | bytes 18874368 | tf_op jit(solution)/shard_map/rf,df->rd/dot_general | solution.py:182
  699.8 15.1 %fusion.38 = bf16[1024,1024]{1,0:T(8,128)(2,1)S(1)} fusion(bf16[4096,1024]{1,0:T(8,128)(2,1)} %get-tuple-element.88, f32[4096,1024]{1,0:T(8,128)} %subtract_multiply_fusion.1), kind=kOutput, calls=%fused_computation.78 | convolution fusion | flops 8595177472 | bytes 27262976 | tf_op jit(solution)/shard_map/rf,rd->fd/dot_general | solution.py:174
  718.4 20.9 %fusion.35 = bf16[1024,1024]{1,0:T(8,128)(2,1)} fusion(bf16[4096,1024]{1,0:T(8,128)(2,1)} %get-tuple-element.110, f32[1024]{0:T(1024)S(1)} %bitcast.146, f32[1024]{0:T(1024)S(1)} %bitcast.135, bf16[4096,1024]{1,0:T(8,128)(2,1)} %all-reduce.10.cloned.1.call-done, bf16[4096,1024]{1,0:T(8,128)(2,1)} %param.13, f32[4096]{0:T(1024)S(1)} %add_rsqrt_fusion.1, ...), kind=kOutput, calls=%fused_computation.77 | convolution fusion | flops 8628731904 | bytes 27308032 | tf_op jit(solution)/shard_map/rd,rf->df/dot_general | solution.py:181
  739.6 113.3 %all-reduce.14.cloned.1.call-done = bf16[4096,1024]{1,0:T(8,128)(2,1)} async-done(((bf16[4096,1024]{1,0:T(8,128)(2,1)}), bf16[4096,1024]{1,0:T(8,128)(2,1)}) %all-reduce.14.cloned.1.call-update) | async-done | bytes 8388624 | tf_op jit(solution)/shard_map/psum | solution.py:183
  852.9 17.3 %multiply_reduce_fusion.2 = (bf16[1024]{0:T(1024)(128)(2,1)S(1)}, f32[4096]{0:T(1024)S(1)}, f32[4096]{0:T(1024)S(1)}, bf16[1024]{0:T(1024)(128)(2,1)S(1)}, bf16[1024]{0:T(1024)(128)(2,1)}) fusion(f32[4096,1024]{1,0:T(8,128)} %subtract_multiply_fusion.1, bf16[4096,1024]{1,0:T(8,128)(2,1)} %all-reduce.14.cloned.1.call-done, f32[4096]{0:T(1024)S(1)} %add_rsqrt_fusion.1, ...), kind=kLoop, calls=%fused_computation.12 | loop fusion | flops 67097600 | bytes 42022912 | tf_op jit(solution)/shard_map/reduce_sum | solution.py:29
  870.2 15.7 %fusion.55 = (bf16[1024]{0:T(1024)(128)(2,1)S(1)}, f32[4096,1024]{1,0:T(8,128)S(1)}) fusion(f32[4096]{0:T(1024)S(1)} %broadcast_multiply_fusion, f32[4096]{0:T(1024)S(1)} %broadcast_multiply_fusion.5, f32[1024]{0:T(1024)S(1)} %bitcast.128, bf16[4096,1024]{1,0:T(8,128)(2,1)} %all-reduce.10.cloned.1.call-done, bf16[4096,1024]{1,0:T(8,128)(2,1)} %param.13, ...), kind=kLoop, calls=%fused_computation.112 | loop fusion | flops 58719232 | bytes 58796032 | tf_op jit(solution)/shard_map/reduce_sum | solution.py:188
  886.0 5.8 copy-done
  903.0 25.9 %multiply_reduce_fusion = (f32[8,4,512]{2,1,0:T(4,128)S(1)}, f32[8,4,512,512]{2,3,1,0:T(8,128)}) fusion(f32[8,4,512]{2,1,0:T(4,128)S(1)} %bitcast.114, f32[8,4,512,512]{2,3,1,0:T(8,128)} %get-tuple-element.101, pred[8,512]{1,0:T(8,128)(4,1)S(1)} %copy-done.12, bf16[8,512,4,64]{1,3,2,0:T(8,128)(2,1)S(1)} %copy.155, bf16[8,512,4,64]{1,3,2,0:T(8,128)(2,1)} %copy.150), kind=kOutput, calls=%fused_computation.1 | convolution fusion | flops 1115668480 | bytes 71438336 | tf_op jit(solution)/shard_map/sihe,sjhe->shij/dot_general | solution.py:55
  928.9 28.6 %multiply_convert_fusion = bf16[8,4,512,512]{2,3,1,0:T(8,128)(2,1)} fusion(f32[8,4,512,512]{2,3,1,0:T(8,128)} %get-tuple-element.104, f32[8,4,512]{2,1,0:T(4,128)S(1)} %get-tuple-element.103, f32[8,4,512]{2,1,0:T(4,128)S(1)} %bitcast.115, f32[8,4,512,512]{2,3,1,0:T(8,128)} %get-tuple-element.101, pred[8,512]{1,0:T(8,128)(4,1)S(1)} %copy-done.12), kind=kLoop, calls=%fused_computation | loop fusion | flops 50331648 | bytes 84021248 | tf_op jit(solution)/shard_map/convert_element_type | solution.py:58
  957.5 12.4 fusion.44
  969.9 8.9 fusion.45
  979.8 10.0 fusion.61
  989.7 16.2 %fusion.60 = (bf16[4,64]{1,0:T(4,128)(2,1)S(1)}, bf16[8,512,4,64]{1,3,2,0:T(8,128)(2,1)}) fusion(bf16[8,512,4,64]{1,3,2,0:T(8,128)(2,1)} %copy-done.8, f32[8,4,512]{2,1,0:T(4,128)S(1)} %bitcast.116, f32[8,4,512,512]{2,3,1,0:T(8,128)} %get-tuple-element.101, pred[8,512]{1,0:T(8,128)(4,1)S(1)} %copy-done.12), kind=kOutput, calls=%fused_computation.116 | convolution fusion | flops 1109393152 | bytes 37818880 | tf_op jit(solution)/shard_map/shij,sihe->sjhe/dot_general | solution.py:66
  1028.1 11.0 convolution_convert_fusion.5
  1041.0 11.3 convolution_convert_fusion
  1060.4 37.6 %all-reduce.4 = (bf16[2,4,64]{2,1,0:T(4,128)(2,1)S(1)}, bf16[1024]{0:T(1024)(128)(2,1)S(1)}, bf16[16,64]{1,0:T(8,128)(2,1)S(1)}, bf16[1024]{0:T(1024)(128)(2,1)S(1)}) all-reduce(bf16[2,4,64]{2,1,0:T(4,128)(2,1)S(1)} %pad_maximum_fusion.2, ...), channel_id=3, replica_groups=mesh['dp'=8,'tensor'=4] {'dp'}, use_global_device_ids=true, to_apply=%region_18.19.clone | all-reduce | flops 3584 | bytes 14336
  1103.8 28.1 %reduce-scatter.25.cloned.1.call-done = bf16[128,2]{1,0:T(8,128)(2,1)} async-done(((bf16[1024,2]{1,0:T(8,128)(2,1)}), bf16[128,2]{1,0:T(8,128)(2,1)}) %reduce-scatter.25.cloned.1.call-update) | async-done | bytes 528
  1133.3 63.0 %reduce-scatter.21.cloned.1.call-done = bf16[128,256]{1,0:T(8,128)(2,1)} async-done(((bf16[1024,256]{1,0:T(8,128)(2,1)}), bf16[128,256]{1,0:T(8,128)(2,1)}) %reduce-scatter.21.cloned.1.call-update) | async-done | bytes 65552
  1197.9 67.1 %reduce-scatter.17.cloned.1.call-done = bf16[3,128,256]{2,1,0:T(8,128)(2,1)} async-done(((bf16[3,1024,256]{2,1,0:T(8,128)(2,1)}), bf16[3,128,256]{2,1,0:T(8,128)(2,1)}) %reduce-scatter.17.cloned.1.call-update) | async-done | bytes 196624 | tf_op jit(solution)/shard_map/reduce_scatter | solution.py:232
  1266.7 152.6 %all-reduce.16.cloned.1.call-done = bf16[4096,1024]{1,0:T(8,128)(2,1)} async-done(((bf16[4096,1024]{1,0:T(8,128)(2,1)}), bf16[4096,1024]{1,0:T(8,128)(2,1)}) %all-reduce.16.cloned.1.call-update) | async-done | bytes 8388624 | tf_op jit(solution)/shard_map/psum | solution.py:218
  1419.2 5.9 dynamic-slice_add_fusion
  (179 shorter events, 87.0 us)
Async XLA Ops:
  7.2 65.7 %all-gather.6.cloned.1.call-start = ((), (), s32[]{:S(2)}) async-start(), calls=%async_computation.6 | async-start | bytes 1769472 | tf_op jit(solution)/shard_map/all_gather | solution.py:106
  9.0 321.5 %all-reduce.10.cloned.1.call-start = ((), (), s32[]{:S(2)}) async-start(), calls=%async_computation.7 | async-start | bytes 16777216 | tf_op jit(solution)/shard_map/psum | solution.py:148
  44.0 109.8 %copy-start.11 = (pred[8,512]{1,0:T(8,128)(4,1)}, pred[8,512]{1,0:T(8,128)(4,1)S(1)}, u32[]{:S(2)}) copy-start(pred[8,512]{1,0:T(8,128)(4,1)S(1)} %get-tuple-element.98) | copy-start | bytes 12292
  72.9 98.0 %copy-start.9 = (bf16[256,1024]{1,0:T(8,128)(2,1)}, bf16[256,1024]{1,0:T(8,128)(2,1)S(1)}, u32[]{:S(2)}) copy-start(bf16[256,1024]{1,0:T(8,128)(2,1)S(1)} %all_gather.37) | copy-start | bytes 1572868
  95.0 43.8 %copy-start.2 = (bf16[8,512,4,64]{1,3,2,0:T(8,128)(2,1)}, bf16[8,512,4,64]{1,3,2,0:T(8,128)(2,1)S(1)}, u32[]{:S(2)}) copy-start(bf16[8,512,4,64]{1,3,2,0:T(8,128)(2,1)S(1)} %copy.148) | copy-start | bytes 6291460
  138.9 15.0 %copy-start.13 = (f32[8,4,512]{2,1,0:T(4,128)}, f32[8,4,512]{2,1,0:T(4,128)S(1)}, u32[]{:S(2)}) copy-start(f32[8,4,512]{2,1,0:T(4,128)S(1)} %get-tuple-element.100) | copy-start | bytes 196612
  138.9 15.0 %copy-start.7 = (bf16[8,512,4,64]{1,3,2,0:T(8,128)(2,1)S(1)}, bf16[8,512,4,64]{1,3,2,0:T(8,128)(2,1)}, u32[]{:S(2)}) copy-start(bf16[8,512,4,64]{1,3,2,0:T(8,128)(2,1)} %copy.150) | copy-start | bytes 6291460
  153.8 14.9 %copy-start.15 = (f32[8,4,512]{2,1,0:T(4,128)}, f32[8,4,512]{2,1,0:T(4,128)S(1)}, u32[]{:S(2)}) copy-start(f32[8,4,512]{2,1,0:T(4,128)S(1)} %fusion) | copy-start | bytes 196612
  168.7 10.4 copy-start.25
  168.8 29.5 %copy-start.26 = (bf16[2,128]{1,0:T(2,128)(2,1)S(1)}, bf16[2,128]{1,0:T(2,128)(2,1)}, u32[]{:S(2)}) copy-start(bf16[2,128]{1,0:T(2,128)(2,1)} %param.23) | copy-start | bytes 1540
  168.8 45.6 %copy-start.27 = (bf16[2,128]{1,0:T(2,128)(2,1)S(1)}, bf16[2,128]{1,0:T(2,128)(2,1)}, u32[]{:S(2)}) copy-start(bf16[2,128]{1,0:T(2,128)(2,1)} %param.24) | copy-start | bytes 1540
  168.8 65.0 %copy-start.23 = (bf16[16,8]{0,1:T(8,128)(2,1)S(1)}, bf16[16,8]{0,1:T(8,128)(2,1)}, u32[]{:S(2)}) copy-start(bf16[16,8]{0,1:T(8,128)(2,1)} %param.20) | copy-start | bytes 772
  177.8 204.3 %all-gather.8.cloned.1.call-start = ((), (), s32[]{:S(2)}) async-start(), calls=%async_computation.8 | async-start | bytes 2359296 | tf_op jit(solution)/shard_map/all_gather | solution.py:110
  178.5 255.1 %all-gather.10.cloned.1.call-start = ((), (), s32[]{:S(2)}) async-start(), calls=%async_computation.9 | async-start | bytes 2359296 | tf_op jit(solution)/shard_map/all_gather | solution.py:112
  179.1 420.7 %all-reduce.12.cloned.1.call-start = ((), (), s32[]{:S(2)}) async-start(), calls=%async_computation.10 | async-start | bytes 16777216 | tf_op jit(solution)/shard_map/psum | solution.py:157
  433.6 15.0 %copy-start.28 = (bf16[128]{0:T(256)(128)(2,1)S(1)}, bf16[128]{0:T(256)(128)(2,1)}, u32[]{:S(2)}) copy-start(bf16[128]{0:T(256)(128)(2,1)} %param.22) | copy-start | bytes 772
  433.6 32.6 %copy-start.17 = (f32[1,4,8,128]{3,2,1,0:T(8,128)S(1)}, f32[1,4,8,128]{3,2,1,0:T(8,128)}, u32[]{:S(2)}) copy-start(f32[1,4,8,128]{3,2,1,0:T(8,128)} %get-tuple-element.99) | copy-start | bytes 49156
  448.5 404.4 %all-reduce.14.cloned.1.call-start = ((), (), s32[]{:S(2)}) async-start(), calls=%async_computation.11 | async-start | bytes 16777216 | tf_op jit(solution)/shard_map/psum | solution.py:183
  599.8 12.6 slice-start.4
  599.8 12.6 slice-start.5
  612.3 12.9 slice-start
  612.4 12.9 slice-start.2
  612.4 12.9 copy-start.18
  612.4 12.8 slice-start.1
  612.4 12.8 slice-start.3
  644.3 13.8 copy-start.1
  658.1 26.7 %copy-start.29 = (bf16[1024,1024]{1,0:T(8,128)(2,1)S(1)}, bf16[1024,1024]{1,0:T(8,128)(2,1)}, u32[]{:S(2)}) copy-start(bf16[1024,1024]{1,0:T(8,128)(2,1)} %all-gather.8.cloned.1.call-done) | copy-start | bytes 6291460
  699.8 18.0 %copy-start.14 = (f32[8,4,512]{2,1,0:T(4,128)S(1)}, f32[8,4,512]{2,1,0:T(4,128)}, u32[]{:S(2)}) copy-start(f32[8,4,512]{2,1,0:T(4,128)} %copy-done.13) | copy-start | bytes 196612
  699.8 18.0 %copy-start.16 = (f32[8,4,512]{2,1,0:T(4,128)S(1)}, f32[8,4,512]{2,1,0:T(4,128)}, u32[]{:S(2)}) copy-start(f32[8,4,512]{2,1,0:T(4,128)} %copy-done.15) | copy-start | bytes 196612
  699.8 358.7 %reduce-scatter.23.cloned.1.call-start = ((), (), s32[]{:S(2)}) async-start(), calls=%async_computation.16 | async-start | bytes 2359296
  717.5 381.2 %reduce-scatter.19.cloned.1.call-start = ((), (), s32[]{:S(2)}) async-start(), calls=%async_computation.14 | async-start | bytes 2359296 | tf_op jit(solution)/shard_map/reduce_scatter | solution.py:244
  739.4 363.0 %reduce-scatter.27.cloned.1.call-start = ((), (), s32[]{:S(2)}) async-start(), calls=%async_computation.18 | async-start | bytes 294912
  870.2 21.5 %copy-start.10 = (bf16[256,1024]{1,0:T(8,128)(2,1)S(1)}, bf16[256,1024]{1,0:T(8,128)(2,1)}, u32[]{:S(2)}) copy-start(bf16[256,1024]{1,0:T(8,128)(2,1)} %copy-done.9) | copy-start | bytes 1572868
  891.8 11.2 copy-start.12
  902.9 25.9 %copy-start.8 = (bf16[8,512,4,64]{1,3,2,0:T(8,128)(2,1)}, bf16[8,512,4,64]{1,3,2,0:T(8,128)(2,1)S(1)}, u32[]{:S(2)}) copy-start(bf16[8,512,4,64]{1,3,2,0:T(8,128)(2,1)S(1)} %copy.155) | copy-start | bytes 6291460
  928.8 28.6 %copy-start.3 = (bf16[8,512,4,64]{1,3,2,0:T(8,128)(2,1)S(1)}, bf16[8,512,4,64]{1,3,2,0:T(8,128)(2,1)}, u32[]{:S(2)}) copy-start(bf16[8,512,4,64]{1,3,2,0:T(8,128)(2,1)} %copy-done.2) | copy-start | bytes 6291460
  969.9 9.9 copy-start.4
  989.7 16.5 %copy-start.21 = (bf16[1,1024]{1,0:T(2,128)(2,1)S(1)}, bf16[1,1024]{1,0:T(2,128)(2,1)}, u32[]{:S(2)}) copy-start(bf16[1,1024]{1,0:T(2,128)(2,1)} %stack.37) | copy-start | bytes 6148
  1006.0 15.4 %copy-start.6 = (bf16[8,512,4,64]{1,3,2,0:T(8,128)(2,1)S(1)}, bf16[8,512,4,64]{1,3,2,0:T(8,128)(2,1)}, u32[]{:S(2)}) copy-start(bf16[8,512,4,64]{1,3,2,0:T(8,128)(2,1)} %fusion.44) | copy-start | bytes 6291460
  1006.0 125.9 %reduce-scatter.25.cloned.1.call-start = ((), (), s32[]{:S(2)}) async-start(), calls=%async_computation.17 | async-start | bytes 294912
  1012.1 184.1 %reduce-scatter.21.cloned.1.call-start = ((), (), s32[]{:S(2)}) async-start(), calls=%async_computation.15 | async-start | bytes 589824
  1023.4 241.6 %reduce-scatter.17.cloned.1.call-start = ((), (), s32[]{:S(2)}) async-start(), calls=%async_computation.13 | async-start | bytes 1769472 | tf_op jit(solution)/shard_map/reduce_scatter | solution.py:232
  1040.6 11.7 copy-start.30
  1040.7 13.6 copy-start.24
  1040.7 13.6 copy-start.19
  1040.7 13.6 copy-start.20
  1040.7 19.7 %copy-start.22 = (bf16[1024]{0:T(1024)(128)(2,1)S(1)}, bf16[1024]{0:T(1024)(128)(2,1)}, u32[]{:S(2)}) copy-start(bf16[1024]{0:T(1024)(128)(2,1)} %get-tuple-element.78) | copy-start | bytes 6148
  1040.7 378.5 %all-reduce.16.cloned.1.call-start = ((), (), s32[]{:S(2)}) async-start(), calls=%async_computation.12 | async-start | bytes 16777216 | tf_op jit(solution)/shard_map/psum | solution.py:218
  (2 other events, 7.1 us)
Sparse Core Ops, SparseCore 0:
  10.6 50.5 all-gather.5
  177.9 152.5 all-reduce.9
  332.7 49.4 all-gather.7
  384.0 49.5 all-gather.9
  448.7 151.0 all-reduce.11
  699.9 152.9 all-reduce.13
  856.5 67.9 reduce-scatter.22
  928.0 66.8 reduce-scatter.18
  1006.1 61.6 reduce-scatter.26
  1071.6 60.2 reduce-scatter.24
  1135.2 60.9 reduce-scatter.20
  1200.5 64.4 reduce-scatter.16
  1267.4 151.7 all-reduce.15
where the time goes:
time: 1440 us; the launch traced here: 1430 us
  waiting for transfers between devices  666 us (46%)
  matrix products  287 us (20%)
  blocking collectives  196 us (14%)
  other arithmetic  173 us (12%)
  local copies, waits for them, and re-layouts  93.4 us (6%)
  between operations  16.1 us (1%)
    psum x1, waiting for transfers between devices, per_device(): lax.psum(in_part.astype(jnp.bfloat16), 'tensor').astype(jnp.float32)  153 us
    psum x1, waiting for transfers between devices, per_device(): lax.psum(ffn_part.astype(jnp.bfloat16), 'tensor').astype(jnp.float32)  134 us
    psum x1, waiting for transfers between devices, per_device(): lax.psum(back_part.astype(jnp.bfloat16), 'tensor').astype(jnp.float32)  113 us
    unnamed x17, waiting for transfers between devices  92.4 us
    psum x1, waiting for transfers between devices, per_device(): lax.psum(attn_part.astype(jnp.bfloat16), 'tensor').astype(jnp.float32)  70.6 us
    reduce_scatter x1, waiting for transfers between devices, per_device(): lax.psum_scatter(qkv_grad.astype(jnp.bfloat16), 'dp', scatter_dimension=1...  67.1 us
    dot_general x1, matrix products, per_device(): jnp.dot(normed_one_b, up_full, preferred_element_type=jnp.float32)  50.2 us
    unnamed x1, blocking collectives  37.6 us
  transfers between devices with their start and end apart: 13, of which 9 were waited for; matrix products, arithmetic and copies ran while one was open for 22% of the time, Pallas kernels for 0%

commit v1 on v0

v1 whole, which is shorter than its diff:
```python
import functools

import jax
import jax.numpy as jnp
from jax import lax
from jax.experimental import pallas as pl
from jax.experimental.pallas import tpu as pltpu
from jax.sharding import PartitionSpec as P

HD = 64
SEQ = 512
EPSILON = 1e-05
SCALE = HD ** (-0.5)
ALL = ("tensor", "dp")
F32 = jnp.float32
BF16 = jnp.bfloat16


def dot(left, right, left_dim, right_dim):
    return lax.dot_general(
        left, right, (((left_dim,), (right_dim,)), ((), ())), preferred_element_type=F32
    )


def head_part(ref, start):
    return ref[0, :, start : start + HD]


def attend_kernel(width, lengths_ref, proj_ref, context_ref, log_ref):
    length = lengths_ref[pl.program_id(1)]
    valid = lax.broadcasted_iota(jnp.int32, (SEQ, SEQ), 0) < length
    done = []
    for head in range(width // HD):
        at = head * HD
        query = head_part(proj_ref, at) * SCALE
        key = head_part(proj_ref, width + at)
        value = head_part(proj_ref, 2 * width + at)
        scores = jnp.where(valid, dot(key, query, 1, 1), -1000000000.0)
        top = jnp.max(scores, axis=0, keepdims=True)
        expo = jnp.exp(scores - top)
        total = jnp.sum(expo, axis=0, keepdims=True)
        probs = (expo * (1.0 / total)).astype(BF16)
        log_ref[0, 0, head : head + 1, :] = top + jnp.log(total)
        done.append(dot(value, probs, 0, 0))
        if len(done) == 2:
            pair = jnp.concatenate(done, axis=0)
            context_ref[0, :, at - HD : at + HD] = pair.T.astype(BF16)
            done = []


def attend_back_kernel(width, lengths_ref, proj_ref, log_ref, d_context_ref, out_ref):
    length = lengths_ref[pl.program_id(1)]
    valid = lax.broadcasted_iota(jnp.int32, (SEQ, SEQ), 0) < length
    d_query, d_key, d_value = [], [], []
    for head in range(width // HD):
        at = head * HD
        query = head_part(proj_ref, at) * SCALE
        key = head_part(proj_ref, width + at)
        value = head_part(proj_ref, 2 * width + at)
        d_context = head_part(d_context_ref, at)
        scores = jnp.where(valid, dot(key, query, 1, 1), -1000000000.0)
        probs = jnp.exp(scores - log_ref[0, 0, head : head + 1, :])
        d_probs = dot(value, d_context, 1, 1)
        inner = jnp.sum(probs * d_probs, axis=0, keepdims=True)
        d_scores = (probs * (d_probs - inner)).astype(BF16)
        d_query.append(dot(key, d_scores, 0, 0) * SCALE)
        d_key.append(dot(d_scores, query, 1, 0).astype(BF16))
        d_value.append(dot(probs.astype(BF16), d_context, 1, 0).astype(BF16))
        if len(d_query) == 2:
            low, high = at - HD, at + HD
            out_ref[0, :, low:high] = jnp.concatenate(d_query, axis=0).T.astype(BF16)
            out_ref[0, :, width + low : width + high] = jnp.concatenate(d_key, axis=1)
            out_ref[0, :, 2 * width + low : 2 * width + high] = jnp.concatenate(d_value, axis=1)
            d_query, d_key, d_value = [], [], []


def attend(lengths, projected):
    groups, rows, joint = projected.shape
    width = joint // 3
    heads = width // HD
    seqs = rows // SEQ
    return pl.pallas_call(
        functools.partial(attend_kernel, width),
        grid=(groups, seqs),
        in_specs=[
            pl.BlockSpec(memory_space=pltpu.SMEM),
            pl.BlockSpec((1, SEQ, joint), lambda t, s: (t, s, 0)),
        ],
        out_specs=[
            pl.BlockSpec((1, SEQ, width), lambda t, s: (t, s, 0)),
            pl.BlockSpec((1, 1, heads, SEQ), lambda t, s: (t, s, 0, 0)),
        ],
        out_shape=[
            jax.ShapeDtypeStruct((groups, rows, width), BF16),
            jax.ShapeDtypeStruct((groups, seqs, heads, SEQ), F32),
        ],
        compiler_params=pltpu.CompilerParams(vmem_limit_bytes=40 * 1024 * 1024),
        cost_estimate=pl.CostEstimate(
            flops=groups * seqs * heads * 16 * SEQ * SEQ * HD,
            bytes_accessed=groups * rows * joint * 3,
            transcendentals=groups * seqs * heads * SEQ * SEQ,
        ),
    )(lengths, projected)


def attend_back(lengths, projected, log_total, d_context):
    groups, rows, joint = projected.shape
    width = joint // 3
    heads = width // HD
    seqs = rows // SEQ
    return pl.pallas_call(
        functools.partial(attend_back_kernel, width),
        grid=(groups, seqs),
        in_specs=[
            pl.BlockSpec(memory_space=pltpu.SMEM),
            pl.BlockSpec((1, SEQ, joint), lambda t, s: (t, s, 0)),
            pl.BlockSpec((1, 1, heads, SEQ), lambda t, s: (t, s, 0, 0)),
            pl.BlockSpec((1, SEQ, width), lambda t, s: (t, s, 0)),
        ],
        out_specs=pl.BlockSpec((1, SEQ, joint), lambda t, s: (t, s, 0)),
        out_shape=jax.ShapeDtypeStruct((groups, rows, joint), BF16),
        compiler_params=pltpu.CompilerParams(vmem_limit_bytes=40 * 1024 * 1024),
        cost_estimate=pl.CostEstimate(
            flops=groups * seqs * heads * 40 * SEQ * SEQ * HD,
            bytes_accessed=groups * rows * joint * 5,
            transcendentals=groups * seqs * heads * SEQ * SEQ,
        ),
    )(lengths, projected, log_total, d_context)


def row_stats(summed):
    row_mean = jnp.mean(summed, axis=-1, keepdims=True)
    centred = summed - row_mean
    inverse = lax.rsqrt(jnp.mean(centred * centred, axis=-1, keepdims=True) + EPSILON)
    return centred * inverse, inverse


def norm_back(grad_rows, unit_rows, inverse, gain_row):
    scaled = grad_rows * gain_row
    inner = (
        scaled
        - jnp.mean(scaled, axis=-1, keepdims=True)
        - unit_rows * jnp.mean(scaled * unit_rows, axis=-1, keepdims=True)
    )
    return (
        inverse * inner,
        jnp.sum(grad_rows * unit_rows, axis=0),
        jnp.sum(grad_rows, axis=0),
    )


def spread(rows, matrices):
    return jnp.einsum("rd,tdn->trn", rows, matrices, preferred_element_type=F32)


def gather_in(parts, matrices):
    return jnp.einsum("trn,tdn->rd", parts, matrices, preferred_element_type=F32)


def outer(rows, parts):
    return jnp.einsum("rd,trn->tdn", rows, parts, preferred_element_type=F32).astype(BF16)


def per_device(
    tokens_all,
    lengths_all,
    qkv_weight,
    qv_bias,
    out_weight,
    out_bias,
    up_weight,
    up_bias,
    down_weight,
    down_bias,
    norm_gain,
    norm_shift,
    cotangent_all,
):
    groups, shares = lax.axis_size("tensor"), lax.axis_size("dp")
    depth, head_width = qkv_weight.shape[1:]
    width = depth * shares
    hidden_width = up_weight.shape[1]
    rows = tokens_all.shape[0] // groups
    seqs = rows // SEQ
    place = lax.axis_index("tensor")
    tokens = lax.dynamic_slice_in_dim(tokens_all, place * rows, rows, 0)
    cotangent = lax.dynamic_slice_in_dim(cotangent_all, place * rows, rows, 0)
    lengths = lax.dynamic_slice_in_dim(lengths_all, place * seqs, seqs, 0)

    def whole(block):
        full = lax.all_gather(block, ALL, axis=0, tiled=True)
        return full.reshape(groups, width, block.shape[1])

    qkv_block = jnp.transpose(qkv_weight, (1, 0, 2)).reshape(depth, 3 * head_width)
    qkv = whole(qkv_block)
    small_shapes = [
        qv_bias.shape, out_bias.shape, up_bias.shape,
        down_bias.shape, norm_gain.shape, norm_shift.shape,
    ]
    small = jnp.concatenate(
        [a.reshape(-1) for a in (qv_bias, out_bias, up_bias, down_bias, norm_gain, norm_shift)]
    )
    smalls = lax.all_gather(small, ALL, axis=0, tiled=False)
    smalls = smalls.reshape(groups, shares, small.shape[0]).astype(F32)
    cut, at = [], 0
    for shape in small_shapes:
        size = 1
        for length in shape:
            size *= length
        cut.append(smalls[:, :, at : at + size].reshape((groups, shares) + shape))
        at += size
    qv = jnp.transpose(cut[0], (0, 2, 3, 1, 4)).reshape(groups, 2, head_width)
    out_shift = cut[1][0].reshape(width)
    up_shift = jnp.transpose(cut[2], (0, 2, 1, 3)).reshape(groups, hidden_width)
    down_shift = cut[3][0].reshape(width)
    gains = jnp.transpose(cut[4][0], (1, 0, 2)).reshape(2, width)
    shifts = jnp.transpose(cut[5][0], (1, 0, 2)).reshape(2, width)

    rest = whole(jnp.concatenate([out_weight.T, up_weight, down_weight.T], axis=1))
    out_full = rest[:, :, :head_width]
    up_full = rest[:, :, head_width : head_width + hidden_width]
    down_full = rest[:, :, head_width + hidden_width :]

    qkv_bias = jnp.concatenate([qv[:, 0], jnp.zeros_like(qv[:, 0]), qv[:, 1]], axis=1)
    projected = (spread(tokens, qkv) + qkv_bias[:, None, :]).astype(BF16)
    context, log_total = attend(lengths, projected)

    attended = gather_in(context, out_full)
    unit_one, inverse_one = row_stats(tokens.astype(F32) + attended + out_shift)
    normed_one = unit_one * gains[0] + shifts[0]
    normed_one_b = normed_one.astype(BF16)
    pre_act = spread(normed_one_b, up_full) + up_shift[:, None, :]
    hidden = jax.nn.gelu(pre_act, approximate=False).astype(BF16)
    ffn_out = gather_in(hidden, down_full)
    unit_two, inverse_two = row_stats(normed_one + ffn_out + down_shift)
    out = (unit_two * gains[1] + shifts[1]).astype(BF16)

    positions = lax.iota(jnp.int32, SEQ)
    row_valid = (positions[None, :] < lengths[:, None]).astype(F32).reshape(rows, 1)
    d_out = cotangent.astype(F32) * row_valid
    d_sum_two, gain_two, shift_two = norm_back(d_out, unit_two, inverse_two, gains[1])
    d_ffn = d_sum_two.astype(BF16)
    down_bias_grad = jnp.sum(d_sum_two, axis=0)

    def owned(grad):
        flat = grad.reshape(groups * width, grad.shape[2])
        return lax.psum_scatter(flat, ALL, scatter_dimension=0, tiled=True).astype(F32)

    down_owned = owned(outer(d_ffn, hidden)).T
    d_hidden = spread(d_ffn, down_full)
    _, gelu_pull = jax.vjp(lambda inner: jax.nn.gelu(inner, approximate=False), pre_act)
    d_pre = gelu_pull(d_hidden)[0].astype(BF16)
    up_bias_grad = jnp.sum(d_pre.astype(F32), axis=1)
    up_grad = outer(normed_one_b, d_pre)
    d_normed_one = d_sum_two + gather_in(d_pre, up_full)
    d_sum_one, gain_one, shift_one = norm_back(d_normed_one, unit_one, inverse_one, gains[0])
    d_attn = d_sum_one.astype(BF16)
    out_bias_grad = jnp.sum(d_sum_one, axis=0)
    out_grad = outer(d_attn, context)
    d_context = spread(d_attn, out_full).astype(BF16)
    d_joined = attend_back(lengths, projected, log_total, d_context)
    qkv_grad = outer(tokens, d_joined)
    rest_owned = owned(jnp.concatenate([up_grad, out_grad, qkv_grad], axis=2))
    up_owned = rest_owned[:, :hidden_width]
    out_owned = rest_owned[:, hidden_width : hidden_width + head_width].T
    qkv_owned = jnp.transpose(
        rest_owned[:, hidden_width + head_width :].reshape(depth, 3, head_width), (1, 0, 2)
    )
    in_grad = d_sum_one + gather_in(d_joined, qkv)

    joined_sums = jnp.sum(d_joined.astype(F32), axis=1).reshape(groups, 3, head_width)
    qv_sums = jnp.stack([joined_sums[:, 0], joined_sums[:, 2]], axis=1)

    def per_owner(array, shape):
        return jnp.broadcast_to(array, (groups, shares) + shape).reshape(groups * shares, -1)

    heads, piece = qv_bias.shape[1:]
    unit_rows, unit_piece = up_bias.shape
    qv_sums = jnp.transpose(qv_sums.reshape(groups, 2, heads, shares, piece), (0, 3, 1, 2, 4))
    up_sums = jnp.transpose(up_bias_grad.reshape(groups, unit_rows, shares, unit_piece), (0, 2, 1, 3))
    two = lambda one, other: jnp.transpose(
        jnp.stack([one, other]).reshape(2, shares, depth), (1, 0, 2)
    )
    to_owners = jnp.concatenate(
        [
            per_owner(qv_sums, qv_bias.shape),
            per_owner(out_bias_grad.reshape(shares, depth), (depth,)),
            per_owner(up_sums, up_bias.shape),
            per_owner(down_bias_grad.reshape(shares, depth), (depth,)),
            per_owner(two(gain_one, gain_two), norm_gain.shape),
            per_owner(two(shift_one, shift_two), norm_shift.shape),
        ],
        axis=1,
    )
    received = lax.all_to_all(to_owners, ALL, 0, 0, tiled=True)
    mine = jnp.sum(received, axis=0)
    small_owned, at = [], 0
    for shape in small_shapes:
        size = 1
        for length in shape:
            size *= length
        small_owned.append(mine[at : at + size].reshape(shape))
        at += size
    qv_owned, outb_owned, upb_owned, downb_owned, gain_owned, shift_owned = small_owned
    return (
        out,
        in_grad,
        qkv_owned,
        qv_owned,
        out_owned,
        outb_owned,
        up_owned,
        upb_owned,
        down_owned,
        downb_owned,
        gain_owned,
        shift_owned,
    )


def solution(mesh):
    in_specs = (
        P("dp", None),
        P("dp"),
        P(None, "dp", "tensor"),
        P(None, "tensor", "dp"),
        P("tensor", "dp"),
        P("dp"),
        P("dp", "tensor"),
        P("tensor", "dp"),
        P("tensor", "dp"),
        P("dp"),
        P(None, "dp"),
        P(None, "dp"),
        P("dp", None),
    )
    out_specs = (
        P(("dp", "tensor"), None),
        P(("dp", "tensor"), None),
        P(None, "dp", "tensor"),
        P(None, "tensor", "dp"),
        P("tensor", "dp"),
        P("dp"),
        P("dp", "tensor"),
        P("tensor", "dp"),
        P("tensor", "dp"),
        P("dp"),
        P(None, "dp"),
        P(None, "dp"),
    )
    return jax.shard_map(
        per_device, mesh=mesh, in_specs=in_specs, out_specs=out_specs, check_vma=False
    )
```

time: 1440 us -> 913 us (0.63)
  waiting for transfers between devices: 666 us -> 472 us
  blocking collectives: 196 us -> 44.5 us
  other arithmetic: 173 us -> 46.8 us
  matrix products: 287 us -> 185 us
  Pallas kernels: 0 us -> 54 us
    psum x4 -> x0, waiting for transfers between devices: 470 us -> none  [the longest x1 153 us: per_device(): lax.psum(in_part.astype(jnp.bfloat16), 'tensor').astype(jnp.float32)]
    reduce_scatter x2 -> x1, waiting for transfers between devices: 67.1 us -> 358 us  [owned(): lax.psum_scatter(flat, ALL, scatter_dimension=0, tiled=True).astype(F32)]
    all_gather x7 -> x0, blocking collectives: 158 us -> none  [the longest x1 32.4 us: per_device(): lax.all_gather(qv_bias, 'dp', axis=2, tiled=True)]
    dot_general x18 -> x12, matrix products: 287 us -> 185 us  [the longest x4 90.9 us: spread(): return jnp.einsum('rd,tdn->trn', rows, matrices, preferred_element_type=F32)]
    unnamed x17 -> x5, waiting for transfers between devices: 92.4 us -> 0.07 us
    all_gather x3 -> x2, waiting for transfers between devices: 35.9 us -> 113 us  [whole(): full = lax.all_gather(block, ALL, axis=0, tiled=True)]
    pallas_call x0 -> x2, Pallas kernels: none -> 54 us  [the longest x1 33.2 us: attend_back(): pl.pallas_call(functools.partial(attend_back_kernel, width), grid=(groups...]
    reshape x8 -> x17, local copies, waits for them, and re-layouts: 45.8 us -> 3.26 us  [the longest x3 1.4 us: per_device(): small_owned.append(mine[at:at + size].reshape(shape))]
  transfers between devices with their start and end apart: 13 -> 5, of which waited for: 9 -> 3; matrix products, arithmetic and copies ran while one was open for 22% -> 20% of each run, Pallas kernels for 0% -> 6%
where the time goes in v1:
time: 913 us; the launch traced here: 904 us
  waiting for transfers between devices  472 us (52%)
  matrix products  185 us (20%)
  local copies, waits for them, and re-layouts  80.9 us (9%)
  Pallas kernels  54 us (6%)
  other arithmetic  46.8 us (5%)
  blocking collectives  44.5 us (5%)
  between operations  15.4 us (2%)
    reduce_scatter x1, waiting for transfers between devices, owned(): lax.psum_scatter(flat, ALL, scatter_dimension=0, tiled=True).astype(F32)  358 us
    all_gather x2, waiting for transfers between devices, whole(): full = lax.all_gather(block, ALL, axis=0, tiled=True)  113 us
    dot_general x4, matrix products, spread(): return jnp.einsum('rd,tdn->trn', rows, matrices, preferred_element_type=F32)  90.9 us
    dot_general x4, matrix products, gather_in(): jnp.einsum('trn,tdn->rd', parts, matrices, preferred_element_type=F32)  49.9 us
    unnamed x1, blocking collectives  44.5 us
    dot_general x4, matrix products, outer(): jnp.einsum('rd,trn->tdn', rows, parts, preferred_element_type=F32)  43.8 us
    pallas_call x1, Pallas kernels, attend_back(): pl.pallas_call(functools.partial(attend_back_kernel, width), grid=(groups...  33.2 us
    all_gather x2, local copies, waits for them, and re-layouts, whole(): full = lax.all_gather(block, ALL, axis=0, tiled=True)  31.4 us
  transfers between devices with their start and end apart: 5, of which 3 were waited for; matrix products, arithmetic and copies ran while one was open for 20% of the time, Pallas kernels for 6%

profile of v1, /device:TPU:0, one launch (start us, length us, event | category | flops | bytes accessed | tf_op | source)
XLA Modules:
  0.0 903.6 jit_solution(15069248981437050692)
XLA Ops:
  7.2 1.7 copy.92
  9.0 1.1 copy.97
  10.2 1.8 pad_maximum_fusion.1
  12.1 0.8 copy.94
  12.9 0.8 reshape.220
  13.7 1.2 dynamic-slice
  15.6 2.8 concatenate.17
  18.6 44.5 %all-reduce = bf16[30720]{0:T(1024)(128)(2,1)S(1)} all-reduce(bf16[30720]{0:T(1024)(128)(2,1)S(1)} %dynamic-update-slice), channel_id=2, replica_groups=mesh['dp'=8,'tensor'=4] {'tensor','dp'}, use_global_device_ids=true, to_apply=%add | all-reduce | flops 30720 | bytes 122880
  64.0 0.7 dynamic_slice.10.lengths_ref
  65.4 0.7 slice_bitcast_fusion.5
  66.7 27.1 %all-gather.4.cloned.1.call-done = bf16[4096,768]{0,1:T(8,128)(2,1)} async-done(((bf16[128,768]{0,1:T(8,128)(2,1)}), bf16[4096,768]{0,1:T(8,128)(2,1)}) %all-gather.4.cloned.1.call-update) | async-done | bytes 6291472 | tf_op jit(solution)/shard_map/all_gather | solution.py:191
  93.8 8.8 copy.93
  102.6 10.0 %fusion.29.proj_ref = bf16[4,1024,768]{2,1,0:T(8,128)(2,1)S(1)} fusion(f32[4,768]{1,0:T(4,128)S(1)} %pad_maximum_fusion.2, bf16[4,1024,768]{2,1,0:T(8,128)(2,1)} %bitcast.239, bf16[4096,1024]{1,0:T(8,128)(2,1)} %param.13, s32[]{:T(128)S(6)} %select_n.7), kind=kOutput, calls=%fused_computation.44 | convolution fusion | flops 6448742400 | bytes 14692356 | tf_op jit(solution)/shard_map/rd,tdn->trn/dot_general | solution.py:153
  112.6 20.8 %shard_map.220 = (bf16[4,1024,256]{2,1,0:T(8,128)(2,1)S(1)}, f32[4,2,4,512]{3,2,1,0:T(4,128)S(1)}) custom-call(s32[2]{0:T(128)S(1)} %dynamic_slice.10.lengths_ref, bf16[4,1024,768]{2,1,0:T(8,128)(2,1)S(1)} %fusion.29.proj_ref), custom_call_target="tpu_custom_call" | custom-call | flops 8589934592 | bytes 9437184 | tf_op jit(solution)/shard_map/pallas_call | solution.py:82
  133.4 2.7 copy-done.3
  136.2 86.1 %all-gather.6.cloned.1.call-done = bf16[4096,2304]{0,1:T(8,128)(2,1)} async-done(((bf16[128,2304]{0,1:T(8,128)(2,1)}), bf16[4096,2304]{0,1:T(8,128)(2,1)}) %all-gather.6.cloned.1.call-update) | async-done | bytes 18874384 | tf_op jit(solution)/shard_map/all_gather | solution.py:191
  222.2 22.7 %copy.98 = bf16[4096,2304]{1,0:T(8,128)(2,1)} copy(bf16[4096,2304]{0,1:T(8,128)(2,1)} %all-gather.6.cloned.1.call-done) | data formatting | bytes 37748736 | tf_op jit(solution)/shard_map/all_gather | solution.py:191
  244.9 4.8 fusion.72
  250.3 51.2 %fusion.9 = (bf16[4,1024,1024]{2,1,0:T(8,128)(2,1)}, f32[4,1024,1024]{2,1,0:T(8,128)}, f32[4,1024,1024]{1,2,0:T(8,128)}) fusion(f32[4,1024]{1,0:T(4,128)S(1)} %add.111, bf16[4,1024,2304]{2,1,0:T(8,128)(2,1)} %bitcast.233, f32[1024,1024]{1,0:T(8,128)S(1)} %get-tuple-element.97, f32[1024]{0:T(1024)S(1)} %get-tuple-element.88, ...), kind=kOutput, calls=%fused_computation.18 | convolution fusion | flops 8872001536 | bytes 54558720 | tf_op jit(solution)/shard_map/rd,tdn->trn/dot_general | solution.py:153
  301.5 14.8 %fusion.73 = (f32[1024]{0:T(1024)S(1)}, f32[1024,1024]{1,0:T(8,128)S(1)}) fusion(f32[1024]{0:T(1024)S(1)} %copy-done.15, bf16[4,1024,1024]{2,1,0:T(8,128)(2,1)} %get-tuple-element.76, bf16[4,1024,2304]{2,1,0:T(8,128)(2,1)} %bitcast.234, f32[1024]{0:T(1024)S(1)} %get-tuple-element.88, f32[1024]{0:T(1024)S(1)} %get-tuple-element.106, ...), kind=kOutput, calls=%fused_computation.131 | convolution fusion | flops 8597273600 | bytes 25190400 | tf_op jit(solution)/shard_map/trn,tdn->rd/dot_general | solution.py:157
  316.9 4.3 multiply_reduce_fusion
  321.3 5.3 fusion.66
  326.6 17.5 %convolution_convert_fusion = bf16[4,1024,1024]{1,2,0:T(8,128)(2,1)} fusion(bf16[4,1024,1024]{2,1,0:T(8,128)(2,1)} %get-tuple-element.76, f32[1024,1024]{1,0:T(8,128)S(1)} %get-tuple-element.73), kind=kOutput, calls=%fused_computation.43 | convolution fusion | flops 8595177472 | bytes 20971520 | tf_op jit(solution)/shard_map/rd,trn->tdn/dot_general | solution.py:161
  344.2 24.2 %convert_reduce_fusion = (f32[4,1024]{1,0:T(4,128)S(1)}, bf16[4,1024,1024]{2,1,0:T(8,128)(2,1)}) fusion(f32[4,1024,1024]{2,1,0:T(8,128)} %get-tuple-element.77, bf16[4,1024,2304]{2,1,0:T(8,128)(2,1)} %bitcast.235, f32[1024,1024]{1,0:T(8,128)} %copy-done.8, f32[4,1024,1024]{1,2,0:T(8,128)} %get-tuple-element.98, f32[4,1024]{1,0:T(4,128)S(1)} %add.111), kind=kOutput, calls=%fused_computation.19 | convolution fusion | flops 8662282240 | bytes 54558720 | tf_op jit(solution)/shard_map/rd,tdn->trn/dot_general | solution.py:153
  368.4 17.7 %multiply_reduce_fusion.1 = (f32[1024]{0:T(1024)S(1)}, f32[1024]{0:T(1024)S(1)}, f32[1024]{0:T(1024)S(1)}, f32[1024]{0:T(1024)S(1)}, f32[1024,1024]{1,0:T(8,128)}) fusion(f32[1024,1024]{1,0:T(8,128)} %copy-done.4, f32[1024]{0:T(1024)S(1)} %add_rsqrt_fusion.1, f32[1024]{0:T(1024)S(1)} %broadcast_multiply_fusion.5, f32[1024]{0:T(1024)S(1)} %get-tuple-element.106, ...), kind=kOutput, calls=%fused_computation.53 | convolution fusion | flops 8600416256 | bytes 29388800 | tf_op jit(solution)/shard_map/trn,tdn->rd/dot_general | solution.py:157
  386.1 3.2 fusion.67
  389.3 5.5 convert_bitcast_fusion.3.d_context_ref
  394.8 3.7 convert_bitcast_fusion.2
  398.5 33.2 %shard_map.221 = bf16[4,1024,768]{2,1,0:T(8,128)(2,1)S(1)} custom-call(s32[2]{0:T(128)S(1)} %dynamic_slice.10.lengths_ref, bf16[4,1024,768]{2,1,0:T(8,128)(2,1)} %copy-done.3, f32[4,2,4,512]{3,2,1,0:T(4,128)S(1)} %get-tuple-element.15.log_ref, bf16[4,1024,256]{2,1,0:T(8,128)(2,1)S(1)} %convert_bitcast_fusion.3.d_context_ref), custom_call_target="tpu_custom_call" | custom-call | flops 21474836480 | bytes 15728640 | tf_op jit(solution)/shard_map/pallas_call | solution.py:111
  431.8 2.6 copy-done
  434.3 10.3 %convert_bitcast_fusion.1 = bf16[4,1024,768]{1,2,0:T(8,128)(2,1)} fusion(bf16[4,1024,768]{2,1,0:T(8,128)(2,1)S(1)} %shard_map.221, bf16[4096,1024]{1,0:T(8,128)(2,1)} %param.13, s32[]{:T(128)S(6)} %select_n.7), kind=kOutput, calls=%fused_computation.45 | convolution fusion | flops 6445596672 | bytes 14680068 | tf_op jit(solution)/shard_map/rd,trn->tdn/dot_general | solution.py:161
  444.6 12.3 %convert_bitcast_fusion = bf16[4,1024,1024]{1,2,0:T(8,128)(2,1)S(1)} fusion(bf16[4,1024,1024]{2,1,0:T(8,128)(2,1)} %get-tuple-element.103, f32[1024,1024]{1,0:T(8,128)S(1)} %copy-done.5, f32[1024]{0:T(1024)S(1)} %get-tuple-element.88, f32[1024]{0:T(1024)S(1)} %get-tuple-element.106, f32[1024]{0:T(1024)S(1)} %add_rsqrt_fusion.1, ...), kind=kOutput, calls=%fused_computation.35 | convolution fusion | flops 8599371776 | bytes 20987904 | tf_op jit(solution)/shard_map/rd,trn->tdn/dot_general | solution.py:161
  456.9 25.2 %pad_maximum_fusion = bf16[4,1024,2048]{1,2,0:T(8,128)(2,1)} fusion(bf16[4,1024,768]{1,2,0:T(8,128)(2,1)S(1)} %copy-done.6, bf16[4,1024,256]{1,2,0:T(8,128)(2,1)} %convert_bitcast_fusion.2, bf16[4,1024,1024]{1,2,0:T(8,128)(2,1)S(1)} %convert_bitcast_fusion), kind=kLoop, calls=%fused_computation.2 | loop fusion | flops 50331648 | bytes 33554432 | tf_op jit(solution)/shard_map/concatenate | solution.py:263
  482.1 21.9 %copy.108 = bf16[4,1024,2048]{2,1,0:T(8,128)(2,1)} copy(bf16[4,1024,2048]{1,2,0:T(8,128)(2,1)} %pad_maximum_fusion) | data formatting | bytes 33554432 | tf_op jit(solution)/shard_map/concatenate | solution.py:263
  504.0 3.7 convert_reduce_fusion.1
  508.6 0.7 all_to_all.6
  509.4 5.7 all-to-all-start
  515.1 12.7 %bitcast_add_fusion = f32[1024,1024]{1,0:T(8,128)} fusion(f32[1024,1024]{1,0:T(8,128)} %copy-done.7, bf16[4,1024,768]{2,1,0:T(8,128)(2,1)} %copy-done, bf16[4,1024,768]{2,1,0:T(8,128)(2,1)} %bitcast.240), kind=kOutput, calls=%fused_computation.46 | convolution fusion | flops 6443499520 | bytes 20971520 | tf_op jit(solution)/shard_map/trn,tdn->rd/dot_general | solution.py:157
  528.5 0.7 copy.116
  529.2 0.7 reshape.241
  530.5 1.1 copy.127
  531.7 0.8 convert_bitcast_fusion.4
  532.5 358.4 %reduce-scatter.5.cloned.1.call-done = bf16[128,2048]{1,0:T(8,128)(2,1)} async-done(((bf16[4096,2048]{1,0:T(8,128)(2,1)}), bf16[128,2048]{1,0:T(8,128)(2,1)}) %reduce-scatter.5.cloned.1.call-update) | async-done | bytes 524304 | tf_op jit(solution)/shard_map/reduce_scatter | solution.py:247
  890.9 1.1 convert_element_type.106
  892.0 0.8 copy.115
  892.8 1.0 slice.151
  893.9 0.9 copy.114
  894.8 1.8 slice.155
  (93 shorter events, 6.4 us)
Async XLA Ops:
  7.2 86.7 %all-gather.4.cloned.1.call-start = ((), (), s32[]{:S(2)}) async-start(), calls=%async_computation.3 | async-start | bytes 6488064 | tf_op jit(solution)/shard_map/all_gather | solution.py:191
  9.0 213.3 %all-gather.6.cloned.1.call-start = ((), (), s32[]{:S(2)}) async-start(), calls=%async_computation.4 | async-start | bytes 19464192 | tf_op jit(solution)/shard_map/all_gather | solution.py:191
  12.0 518.5 %reduce-scatter.7.cloned.1.call-start = ((), (), s32[]{:S(2)}) async-start(), calls=%async_computation.6 | async-start | bytes 8650752
  133.4 2.8 copy-start.3
  136.2 108.8 %copy-start.1 = (bf16[4,1024,256]{2,1,0:T(8,128)(2,1)}, bf16[4,1024,256]{2,1,0:T(8,128)(2,1)S(1)}, u32[]{:S(2)}) copy-start(bf16[4,1024,256]{2,1,0:T(8,128)(2,1)S(1)} %get-tuple-element.14) | copy-start | bytes 6291460
  249.7 51.8 %copy-start.4 = (f32[1024,1024]{1,0:T(8,128)}, f32[1024,1024]{1,0:T(8,128)S(1)}, u32[]{:S(2)}) copy-start(f32[1024,1024]{1,0:T(8,128)S(1)} %get-tuple-element.97) | copy-start | bytes 12582916
  250.3 51.2 %copy-start.15 = (f32[1024]{0:T(1024)S(1)}, f32[1024]{0:T(1024)}, u32[]{:S(2)}) copy-start(f32[1024]{0:T(1024)} %get-tuple-element.79) | copy-start | bytes 12292
  301.5 15.4 %copy-start.9 = (f32[1,4,2,128]{3,1,2,0:T(4,128)S(1)}, f32[1,4,2,128]{3,1,2,0:T(4,128)}, u32[]{:S(2)}) copy-start(f32[1,4,2,128]{3,1,2,0:T(4,128)} %copy.130) | copy-start | bytes 12292
  301.5 15.4 %copy-start.10 = (f32[1024]{0:T(1024)S(1)}, f32[1024]{0:T(1024)}, u32[]{:S(2)}) copy-start(f32[1024]{0:T(1024)} %get-tuple-element.107) | copy-start | bytes 12292
  316.3 5.0 copy-start.12
  326.6 17.6 %copy-start.8 = (f32[1024,1024]{1,0:T(8,128)}, f32[1024,1024]{1,0:T(8,128)S(1)}, u32[]{:S(2)}) copy-start(f32[1024,1024]{1,0:T(8,128)S(1)} %get-tuple-element.73) | copy-start | bytes 12582916
  344.1 546.7 %reduce-scatter.5.cloned.1.call-start = ((), (), s32[]{:S(2)}) async-start(), calls=%async_computation.5 | async-start | bytes 17301504 | tf_op jit(solution)/shard_map/reduce_scatter | solution.py:247
  368.4 17.7 %copy-start.5 = (f32[1024,1024]{1,0:T(8,128)S(1)}, f32[1024,1024]{1,0:T(8,128)}, u32[]{:S(2)}) copy-start(f32[1024,1024]{1,0:T(8,128)} %copy-done.4) | copy-start | bytes 12582916
  389.3 9.2 %copy-start.7 = (f32[1024,1024]{1,0:T(8,128)}, f32[1024,1024]{1,0:T(8,128)S(1)}, u32[]{:S(2)}) copy-start(f32[1024,1024]{1,0:T(8,128)S(1)} %get-tuple-element.75) | copy-start | bytes 12582916
  389.3 5.5 copy-start.2
  431.8 2.6 copy-start
  444.6 12.3 %copy-start.6 = (bf16[4,1024,768]{1,2,0:T(8,128)(2,1)S(1)}, bf16[4,1024,768]{1,2,0:T(8,128)(2,1)}, u32[]{:S(2)}) copy-start(bf16[4,1024,768]{1,2,0:T(8,128)(2,1)} %convert_bitcast_fusion.1) | copy-start | bytes 18874372
  504.0 4.4 copy-start.14
  504.0 4.4 copy-start.13
  504.0 4.4 copy-start.11
  509.4 18.4 %all-to-all-start = ((f32[32,1,960]{2,1,0:T(1,128)}), f32[32,1,960]{2,1,0:T(1,128)S(1)}, u32[]{:S(2)}, u32[]{:S(2)}) async-start(f32[32,1,960]{2,1,0:T(1,128)} %all_to_all.6), calls=%async_computation.1 | async-start | bytes 262144 | tf_op jit(solution)/shard_map/all_to_all | solution.py:295
Sparse Core Ops, SparseCore 0:
  11.4 82.3 all-gather.3
  95.9 126.3 all-gather.5
  344.3 186.0 reduce-scatter.6
  532.5 358.2 reduce-scatter.4

commit v2 on v1

--- a/solution.py
+++ b/solution.py
@@ -243,8 +243,11 @@
     down_bias_grad = jnp.sum(d_sum_two, axis=0)
 
     def owned(grad):
-        flat = grad.reshape(groups * width, grad.shape[2])
-        return lax.psum_scatter(flat, ALL, scatter_dimension=0, tiled=True).astype(F32)
+        blocks = grad.reshape(groups, shares, depth, grad.shape[2])
+        flat = jnp.transpose(blocks, (1, 0, 2, 3)).reshape(groups * width, grad.shape[2])
+        return lax.psum_scatter(
+            flat, ("dp", "tensor"), scatter_dimension=0, tiled=True
+        ).astype(F32)
 
     down_owned = owned(outer(d_ffn, hidden)).T
     d_hidden = spread(d_ffn, down_full)

time: 913 us -> 724 us (0.79)
  waiting for transfers between devices: 472 us -> 269 us
  local copies, waits for them, and re-layouts: 80.9 us -> 99.5 us
    reduce_scatter x1 -> x0, waiting for transfers between devices: 358 us -> none  [owned(): lax.psum_scatter(flat, ALL, scatter_dimension=0, tiled=True).astype(F32)]
    unnamed x5 -> x6, waiting for transfers between devices: 0.07 us -> 156 us
    unnamed x43 -> x51, local copies, waits for them, and re-layouts: 14.6 us -> 57.3 us
    concatenate x1 -> x0, local copies, waits for them, and re-layouts: 21.9 us -> none  [per_device(): rest_owned = owned(jnp.concatenate([up_grad, out_grad, qkv_grad], axis=2))]
  transfers between devices with their start and end apart: 5 -> 5, of which waited for: 3 -> 3; matrix products, arithmetic and copies ran while one was open for 20% -> 26% of each run, Pallas kernels for 6% -> 8%
where the time goes in v2:
time: 724 us; the launch traced here: 713 us
  waiting for transfers between devices  269 us (37%)
  matrix products  184 us (25%)
  local copies, waits for them, and re-layouts  99.5 us (14%)
  Pallas kernels  54.5 us (8%)
  blocking collectives  44.5 us (6%)
  other arithmetic  40.2 us (6%)
  between operations  15.5 us (2%)
    unnamed x6, waiting for transfers between devices  156 us
    all_gather x2, waiting for transfers between devices, whole(): full = lax.all_gather(block, ALL, axis=0, tiled=True)  113 us
    dot_general x4, matrix products, spread(): return jnp.einsum('rd,tdn->trn', rows, matrices, preferred_element_type=F32)  91.3 us
    unnamed x51, local copies, waits for them, and re-layouts  57.3 us
    dot_general x4, matrix products, gather_in(): jnp.einsum('trn,tdn->rd', parts, matrices, preferred_element_type=F32)  48.8 us
    unnamed x1, blocking collectives  44.5 us
    dot_general x4, matrix products, outer(): jnp.einsum('rd,trn->tdn', rows, parts, preferred_element_type=F32)  44 us
    pallas_call x1, Pallas kernels, attend_back(): pl.pallas_call(functools.partial(attend_back_kernel, width), grid=(groups...  33.4 us
  transfers between devices with their start and end apart: 5, of which 3 were waited for; matrix products, arithmetic and copies ran while one was open for 26% of the time, Pallas kernels for 8%

profile of v2, /device:TPU:0, one launch (start us, length us, event | category | flops | bytes accessed | tf_op | source)
XLA Modules:
  0.0 712.7 jit_solution(10157384477897069455)
XLA Ops:
  7.2 1.7 copy.91
  9.0 1.1 copy.96
  10.2 1.8 pad_maximum_fusion.1
  12.1 0.8 copy.93
  12.9 0.8 reshape.226
  13.7 1.2 dynamic-slice
  15.6 2.8 concatenate.17
  18.6 44.5 %all-reduce = bf16[30720]{0:T(1024)(128)(2,1)S(1)} all-reduce(bf16[30720]{0:T(1024)(128)(2,1)S(1)} %dynamic-update-slice), channel_id=2, replica_groups=mesh['dp'=8,'tensor'=4] {'tensor','dp'}, use_global_device_ids=true, to_apply=%add | all-reduce | flops 30720 | bytes 122880
  64.0 0.7 dynamic_slice.10.lengths_ref
  66.7 27.1 %all-gather.4.cloned.1.call-done = bf16[4096,768]{0,1:T(8,128)(2,1)} async-done(((bf16[128,768]{0,1:T(8,128)(2,1)}), bf16[4096,768]{0,1:T(8,128)(2,1)}) %all-gather.4.cloned.1.call-update) | async-done | bytes 6291472 | tf_op jit(solution)/shard_map/all_gather | solution.py:191
  93.8 8.8 %copy.92 = bf16[4096,768]{1,0:T(8,128)(2,1)} copy(bf16[4096,768]{0,1:T(8,128)(2,1)} %all-gather.4.cloned.1.call-done) | data formatting | bytes 12582912 | tf_op jit(solution)/shard_map/all_gather | solution.py:191
  102.6 10.0 %fusion.29.proj_ref = bf16[4,1024,768]{2,1,0:T(8,128)(2,1)S(1)} fusion(f32[4,768]{1,0:T(4,128)S(1)} %pad_maximum_fusion.2, bf16[4,1024,768]{2,1,0:T(8,128)(2,1)} %bitcast.254, bf16[4096,1024]{1,0:T(8,128)(2,1)} %param.13, s32[]{:T(128)S(6)} %select_n.7), kind=kOutput, calls=%fused_computation.44 | convolution fusion | flops 6448742400 | bytes 14692356 | tf_op jit(solution)/shard_map/rd,tdn->trn/dot_general | solution.py:153
  112.6 21.1 %shard_map.220 = (bf16[4,1024,256]{2,1,0:T(8,128)(2,1)S(1)}, f32[4,2,4,512]{3,2,1,0:T(4,128)S(1)}) custom-call(s32[2]{0:T(128)S(1)} %dynamic_slice.10.lengths_ref, bf16[4,1024,768]{2,1,0:T(8,128)(2,1)S(1)} %fusion.29.proj_ref), custom_call_target="tpu_custom_call" | custom-call | flops 8589934592 | bytes 9437184 | tf_op jit(solution)/shard_map/pallas_call | solution.py:82
  133.7 2.7 copy-done.3
  136.5 85.7 %all-gather.6.cloned.1.call-done = bf16[4096,2304]{0,1:T(8,128)(2,1)} async-done(((bf16[128,2304]{0,1:T(8,128)(2,1)}), bf16[4096,2304]{0,1:T(8,128)(2,1)}) %all-gather.6.cloned.1.call-update) | async-done | bytes 18874384 | tf_op jit(solution)/shard_map/all_gather | solution.py:191
  222.2 22.7 %copy.97 = bf16[4096,2304]{1,0:T(8,128)(2,1)} copy(bf16[4096,2304]{0,1:T(8,128)(2,1)} %all-gather.6.cloned.1.call-done) | data formatting | bytes 37748736 | tf_op jit(solution)/shard_map/all_gather | solution.py:191
  244.9 4.9 fusion.72
  250.4 51.5 %fusion.9 = (bf16[4,1024,1024]{2,1,0:T(8,128)(2,1)}, f32[4,1024,1024]{2,1,0:T(8,128)}, f32[4,1024,1024]{1,2,0:T(8,128)}) fusion(f32[4,1024]{1,0:T(4,128)S(1)} %add.111, bf16[4,1024,2304]{2,1,0:T(8,128)(2,1)} %bitcast.248, f32[1024,1024]{1,0:T(8,128)S(1)} %get-tuple-element.97, f32[1024]{0:T(1024)S(1)} %get-tuple-element.88, ...), kind=kOutput, calls=%fused_computation.18 | convolution fusion | flops 8872001536 | bytes 54558720 | tf_op jit(solution)/shard_map/rd,tdn->trn/dot_general | solution.py:153
  302.0 14.8 %fusion.73 = (f32[1024]{0:T(1024)S(1)}, f32[1024,1024]{1,0:T(8,128)S(1)}) fusion(f32[1024]{0:T(1024)S(1)} %copy-done.15, bf16[4,1024,1024]{2,1,0:T(8,128)(2,1)} %get-tuple-element.76, bf16[4,1024,2304]{2,1,0:T(8,128)(2,1)} %bitcast.249, f32[1024]{0:T(1024)S(1)} %get-tuple-element.88, f32[1024]{0:T(1024)S(1)} %get-tuple-element.106, ...), kind=kOutput, calls=%fused_computation.131 | convolution fusion | flops 8597273600 | bytes 25190400 | tf_op jit(solution)/shard_map/trn,tdn->rd/dot_general | solution.py:157
  317.4 3.2 multiply_reduce_fusion
  320.6 3.7 fusion.66
  324.3 17.5 %convolution_convert_fusion = bf16[4,1024,1024]{1,2,0:T(8,128)(2,1)} fusion(bf16[4,1024,1024]{2,1,0:T(8,128)(2,1)} %get-tuple-element.76, f32[1024,1024]{1,0:T(8,128)S(1)} %get-tuple-element.73), kind=kOutput, calls=%fused_computation.43 | convolution fusion | flops 8595177472 | bytes 20971520 | tf_op jit(solution)/shard_map/rd,trn->tdn/dot_general | solution.py:161
  341.8 8.3 %copy.129 = bf16[8,4,128,1024]{3,2,1,0:T(8,128)(2,1)} copy(bf16[8,4,128,1024]{3,2,0,1:T(8,128)(2,1)} %bitcast.253) | data formatting | bytes 16777216
  350.1 24.3 %convert_reduce_fusion = (f32[4,1024]{1,0:T(4,128)S(1)}, bf16[4,1024,1024]{2,1,0:T(8,128)(2,1)}) fusion(f32[4,1024,1024]{2,1,0:T(8,128)} %get-tuple-element.77, bf16[4,1024,2304]{2,1,0:T(8,128)(2,1)} %bitcast.250, f32[1024,1024]{1,0:T(8,128)} %copy-done.8, f32[4,1024,1024]{1,2,0:T(8,128)} %get-tuple-element.98, f32[4,1024]{1,0:T(4,128)S(1)} %add.111), kind=kOutput, calls=%fused_computation.19 | convolution fusion | flops 8662282240 | bytes 54558720 | tf_op jit(solution)/shard_map/rd,tdn->trn/dot_general | solution.py:153
  374.4 16.4 %multiply_reduce_fusion.1 = (f32[1024]{0:T(1024)S(1)}, f32[1024]{0:T(1024)S(1)}, f32[1024]{0:T(1024)S(1)}, f32[1024]{0:T(1024)S(1)}, f32[1024,1024]{1,0:T(8,128)S(1)}) fusion(f32[1024,1024]{1,0:T(8,128)} %copy-done.4, f32[1024]{0:T(1024)S(1)} %add_rsqrt_fusion.1, f32[1024]{0:T(1024)S(1)} %broadcast_multiply_fusion.5, f32[1024]{0:T(1024)S(1)} %get-tuple-element.106, ...), kind=kOutput, calls=%fused_computation.53 | convolution fusion | flops 8600416256 | bytes 29388800 | tf_op jit(solution)/shard_map/trn,tdn->rd/dot_general | solution.py:157
  390.8 1.6 fusion.67
  392.5 5.5 convert_bitcast_fusion.3.d_context_ref
  398.0 3.8 convert_bitcast_fusion.2
  401.7 33.4 %shard_map.221 = bf16[4,1024,768]{2,1,0:T(8,128)(2,1)S(1)} custom-call(s32[2]{0:T(128)S(1)} %dynamic_slice.10.lengths_ref, bf16[4,1024,768]{2,1,0:T(8,128)(2,1)} %copy-done.3, f32[4,2,4,512]{3,2,1,0:T(4,128)S(1)} %get-tuple-element.15.log_ref, bf16[4,1024,256]{2,1,0:T(8,128)(2,1)S(1)} %convert_bitcast_fusion.3.d_context_ref), custom_call_target="tpu_custom_call" | custom-call | flops 21474836480 | bytes 15728640 | tf_op jit(solution)/shard_map/pallas_call | solution.py:111
  435.1 2.6 copy-done
  437.7 10.3 %convert_bitcast_fusion.1 = bf16[4,1024,768]{1,2,0:T(8,128)(2,1)} fusion(bf16[4,1024,768]{2,1,0:T(8,128)(2,1)S(1)} %shard_map.221, bf16[4096,1024]{1,0:T(8,128)(2,1)} %param.13, s32[]{:T(128)S(6)} %select_n.7), kind=kOutput, calls=%fused_computation.45 | convolution fusion | flops 6445596672 | bytes 14680068 | tf_op jit(solution)/shard_map/rd,trn->tdn/dot_general | solution.py:161
  448.0 12.4 %convert_bitcast_fusion = bf16[4,1024,1024]{1,2,0:T(8,128)(2,1)S(1)} fusion(bf16[4,1024,1024]{2,1,0:T(8,128)(2,1)} %get-tuple-element.103, f32[1024,1024]{1,0:T(8,128)S(1)} %copy-done.5, f32[1024]{0:T(1024)S(1)} %get-tuple-element.88, f32[1024]{0:T(1024)S(1)} %get-tuple-element.106, f32[1024]{0:T(1024)S(1)} %add_rsqrt_fusion.1, ...), kind=kOutput, calls=%fused_computation.35 | convolution fusion | flops 8599371776 | bytes 20987904 | tf_op jit(solution)/shard_map/rd,trn->tdn/dot_general | solution.py:161
  460.5 24.1 %pad_maximum_fusion = bf16[4,1024,2048]{1,2,0:T(8,128)(2,1)S(1)} fusion(bf16[4,1024,768]{1,2,0:T(8,128)(2,1)S(1)} %copy-done.6, bf16[4,1024,256]{1,2,0:T(8,128)(2,1)} %convert_bitcast_fusion.2, bf16[4,1024,1024]{1,2,0:T(8,128)(2,1)S(1)} %convert_bitcast_fusion), kind=kLoop, calls=%fused_computation.2 | loop fusion | flops 50331648 | bytes 33554432 | tf_op jit(solution)/shard_map/concatenate | solution.py:266
  484.6 9.1 %copy.135 = bf16[1024,8,8,128]{3,2,1,0:T(8,128)(2,1)} copy(bf16[1024,8,8,128]{3,1,2,0:T(8,128)(2,1)S(1)} %bitcast.244) | data formatting | bytes 33554432
  493.6 23.8 %copy.128 = bf16[8,4,128,2048]{3,2,1,0:T(8,128)(2,1)} copy(bf16[8,4,128,2048]{2,0,3,1:T(8,128)(2,1)} %bitcast.245) | data formatting | bytes 33554432
  517.4 3.6 convert_reduce_fusion.1
  522.0 0.7 all_to_all.6
  522.7 5.8 all-to-all-start
  528.5 12.7 %bitcast_add_fusion = f32[1024,1024]{1,0:T(8,128)} fusion(f32[1024,1024]{1,0:T(8,128)} %copy-done.7, bf16[4,1024,768]{2,1,0:T(8,128)(2,1)} %copy-done, bf16[4,1024,768]{2,1,0:T(8,128)(2,1)} %bitcast.255), kind=kOutput, calls=%fused_computation.46 | convolution fusion | flops 6443499520 | bytes 20971520 | tf_op jit(solution)/shard_map/trn,tdn->rd/dot_general | solution.py:157
  541.9 0.7 copy.114
  542.6 0.7 reshape.248
  543.9 1.1 copy.127
  545.1 0.8 convert_bitcast_fusion.4
  545.9 155.7 %reduce-scatter.7.cloned.1.call-done = bf16[128,2048]{1,0:T(8,128)(2,1)} async-done(((bf16[4096,2048]{1,0:T(8,128)(2,1)}), bf16[128,2048]{1,0:T(8,128)(2,1)}) %reduce-scatter.7.cloned.1.call-update) | async-done | bytes 524304
  701.6 1.3 copy.125
  703.1 0.7 slice_bitcast_fusion
  703.8 1.0 copy.113
  704.8 0.9 copy.112
  (100 shorter events, 7.0 us)
Async XLA Ops:
  7.2 86.7 %all-gather.4.cloned.1.call-start = ((), (), s32[]{:S(2)}) async-start(), calls=%async_computation.3 | async-start | bytes 6488064 | tf_op jit(solution)/shard_map/all_gather | solution.py:191
  9.0 213.2 %all-gather.6.cloned.1.call-start = ((), (), s32[]{:S(2)}) async-start(), calls=%async_computation.4 | async-start | bytes 19464192 | tf_op jit(solution)/shard_map/all_gather | solution.py:191
  12.0 531.9 %reduce-scatter.9.cloned.1.call-start = ((), (), s32[]{:S(2)}) async-start(), calls=%async_computation.6 | async-start | bytes 8650752
  133.7 2.8 copy-start.3
  136.5 108.4 %copy-start.1 = (bf16[4,1024,256]{2,1,0:T(8,128)(2,1)}, bf16[4,1024,256]{2,1,0:T(8,128)(2,1)S(1)}, u32[]{:S(2)}) copy-start(bf16[4,1024,256]{2,1,0:T(8,128)(2,1)S(1)} %get-tuple-element.14) | copy-start | bytes 6291460
  244.9 72.5 %slice-start = ((s8[8388608]{0:T(1024)(128)(4,1)}), s8[4194304]{0:T(1024)(128)(4,1)S(1)}, s32[]{:S(2)}) async-start(s8[8388608]{0:T(1024)(128)(4,1)} %bitcast.256), calls=%async_computation.7 | async-start | bytes 8388608
  249.8 52.1 %copy-start.4 = (f32[1024,1024]{1,0:T(8,128)}, f32[1024,1024]{1,0:T(8,128)S(1)}, u32[]{:S(2)}) copy-start(f32[1024,1024]{1,0:T(8,128)S(1)} %get-tuple-element.97) | copy-start | bytes 12582916
  250.4 51.5 %copy-start.15 = (f32[1024]{0:T(1024)S(1)}, f32[1024]{0:T(1024)}, u32[]{:S(2)}) copy-start(f32[1024]{0:T(1024)} %get-tuple-element.79) | copy-start | bytes 12292
  250.4 67.0 %slice-start.1 = ((s8[8388608]{0:T(1024)(128)(4,1)}), s8[4194304]{0:T(1024)(128)(4,1)S(1)}, s32[]{:S(2)}) async-start(s8[8388608]{0:T(1024)(128)(4,1)} %bitcast.256), calls=%async_computation.8 | async-start | bytes 8388608
  301.9 15.4 %copy-start.9 = (f32[1,4,2,128]{3,1,2,0:T(4,128)S(1)}, f32[1,4,2,128]{3,1,2,0:T(4,128)}, u32[]{:S(2)}) copy-start(f32[1,4,2,128]{3,1,2,0:T(4,128)} %copy.134) | copy-start | bytes 12292
  301.9 15.4 %copy-start.10 = (f32[1024]{0:T(1024)S(1)}, f32[1024]{0:T(1024)}, u32[]{:S(2)}) copy-start(f32[1024]{0:T(1024)} %get-tuple-element.107) | copy-start | bytes 12292
  316.7 3.9 copy-start.12
  324.3 17.5 %copy-start.8 = (f32[1024,1024]{1,0:T(8,128)}, f32[1024,1024]{1,0:T(8,128)S(1)}, u32[]{:S(2)}) copy-start(f32[1024,1024]{1,0:T(8,128)S(1)} %get-tuple-element.73) | copy-start | bytes 12582916
  350.1 351.5 %reduce-scatter.7.cloned.1.call-start = ((), (), s32[]{:S(2)}) async-start(), calls=%async_computation.5 | async-start | bytes 17301504
  374.4 16.4 %copy-start.5 = (f32[1024,1024]{1,0:T(8,128)S(1)}, f32[1024,1024]{1,0:T(8,128)}, u32[]{:S(2)}) copy-start(f32[1024,1024]{1,0:T(8,128)} %copy-done.4) | copy-start | bytes 12582916
  392.4 9.3 %copy-start.7 = (f32[1024,1024]{1,0:T(8,128)}, f32[1024,1024]{1,0:T(8,128)S(1)}, u32[]{:S(2)}) copy-start(f32[1024,1024]{1,0:T(8,128)S(1)} %get-tuple-element.75) | copy-start | bytes 12582916
  392.5 5.5 copy-start.2
  435.1 2.6 copy-start
  448.0 12.4 %copy-start.6 = (bf16[4,1024,768]{1,2,0:T(8,128)(2,1)S(1)}, bf16[4,1024,768]{1,2,0:T(8,128)(2,1)}, u32[]{:S(2)}) copy-start(bf16[4,1024,768]{1,2,0:T(8,128)(2,1)} %convert_bitcast_fusion.1) | copy-start | bytes 18874372
  517.4 4.4 copy-start.14
  517.4 4.4 copy-start.13
  517.4 4.4 copy-start.11
  522.7 18.4 %all-to-all-start = ((f32[32,1,960]{2,1,0:T(1,128)}), f32[32,1,960]{2,1,0:T(1,128)S(1)}, u32[]{:S(2)}, u32[]{:S(2)}) async-start(f32[32,1,960]{2,1,0:T(1,128)} %all_to_all.6), calls=%async_computation | async-start | bytes 262144 | tf_op jit(solution)/shard_map/all_to_all | solution.py:298
Sparse Core Ops, SparseCore 0:
  11.4 82.3 all-gather.3
  95.9 126.2 all-gather.5
  350.2 149.5 reduce-scatter.8
  517.6 184.0 reduce-scatter.6
